TPU v7x, 32 devices: a whole 2x2x4 slice. The times are simulated.
32 devices in a mesh: ctx: 16 (over z, x, core), ch: 2 (over y).
Axes of the slice: x: 2, y: 2, z: 4, core: 2. Of those that a mesh axis runs over, the one named last changes fastest.
Arguments:
- grad_out: bfloat16 [2048, 4096], P('ctx', 'ch'), may hold values from -6 to 6
- inputs: bfloat16 [2048, 4096], P('ctx', 'ch'), may hold values from -0.3125 to 0.3125
- filter_taps: bfloat16 [128, 8, 4096], P('ctx', 'ch'), may hold values from -0.1875 to 0.1875
Outputs:
- grad_inputs: bfloat16 [2048, 4096], P('ctx', 'ch')
- grad_taps: float32 [128, 8, 4096], P('ctx', 'ch')
All inputs are finite; a program needn't handle non-finite values.
Results may differ from a plain program's by a relative error of at most 0.0085.
Values may be sent and summed in bfloat16 or wider, within the bound.
No kernel may reach another device: no remote copies, remote signals or barrier semaphores. Data moves between devices by JAX's collectives and lax.ppermute only.
A program may use at most 128 MiB of HBM per device.

v0:
```python
import math

import jax
import jax.numpy as jnp
from jax import lax
from jax.sharding import PartitionSpec as P

HIGH_PREC = lax.Precision.HIGH


def passed_along(block, axis, distance):
    devices = range(lax.axis_size(axis))
    route = [(i - distance, i) for i in devices if i - distance in devices]
    return lax.ppermute(block, axis, route)


def split_table(table):
    upper = table.astype(jnp.bfloat16)
    lower = (table - upper.astype(jnp.float32)).astype(jnp.bfloat16)
    return (upper, lower)


def dft_tables(block_rows):
    freq_index = lax.broadcasted_iota(jnp.int32, (block_rows, block_rows), 0)
    place_index = lax.broadcasted_iota(jnp.int32, (block_rows, block_rows), 1)
    phase_index = freq_index * place_index % (2 * block_rows)
    angles = phase_index.astype(jnp.float32) * jnp.float32(math.pi / block_rows)
    cosine = jnp.cos(angles)
    sine_table = jnp.sin(angles)
    col_parity = jnp.where(place_index % 2 == 0, 1.0, -1.0).astype(jnp.float32)
    row_parity = jnp.where(freq_index % 2 == 0, 1.0, -1.0).astype(jnp.float32)
    scale_inv = jnp.float32(0.5 / block_rows)
    fwd_real = jnp.where(freq_index == 0, 1.0, cosine)
    fwd_imag = jnp.where(freq_index == 0, col_parity, -sine_table)
    inv_real = jnp.where(place_index == 0, 1.0, 2.0 * cosine) * scale_inv
    inv_imag = jnp.where(place_index == 0, row_parity, -2.0 * sine_table) * scale_inv
    parity = row_parity[:, :1]
    dc_row = freq_index[:, :1] == 0
    return (split_table(fwd_real), split_table(fwd_imag), inv_real, inv_imag, parity, dc_row)


def split_dot(pair, signal):
    first = jnp.dot(pair[0], signal, preferred_element_type=jnp.float32)
    return first + jnp.dot(pair[1], signal, preferred_element_type=jnp.float32)


def spectrum(tables, signal):
    return (split_dot(tables[0], signal), split_dot(tables[1], signal))


def inverse(tables, spec):
    first_half = jnp.dot(
        tables[2], spec[0], precision=HIGH_PREC, preferred_element_type=jnp.float32
    )
    return first_half + jnp.dot(
        tables[3], spec[1], precision=HIGH_PREC, preferred_element_type=jnp.float32
    )


def conj_product(dc_row, left, right):
    left_real, left_imag = left
    right_real, right_imag = right
    both_imag = left_imag * right_imag
    real_part = left_real * right_real + jnp.where(dc_row, 0.0, both_imag)
    imag_part = jnp.where(dc_row, both_imag, left_real * right_imag - left_imag * right_real)
    return (real_part, imag_part)


def signed_sum(parity, first_spec, second_spec):
    return (first_spec[0] + parity * second_spec[0], first_spec[1] + parity * second_spec[1])


def reduce_segment(tables, spec):
    return lax.psum_scatter(inverse(tables, spec), "ctx", scatter_dimension=0, tiled=True)


def shards(grad_out, inputs, filter_taps):
    block_rows = grad_out.shape[0]
    segments = filter_taps.shape[1] * lax.axis_size("ch")
    seq_blocks = lax.axis_size("ctx")
    tables = dft_tables(block_rows)
    parity = tables[4]
    dc_row = tables[5]
    position = lax.axis_index("ctx")
    own_taps = lax.all_to_all(filter_taps, "ch", split_axis=2, concat_axis=1, tiled=True)
    all_taps = lax.all_gather(own_taps, "ctx", axis=0, tiled=True)
    value_spec = spectrum(tables, inputs)
    width = grad_out.shape[1]
    zero_spec = (
        jnp.zeros((block_rows, width), jnp.float32),
        jnp.zeros((block_rows, width), jnp.float32),
    )
    input_grad_spec = zero_spec
    prev_grad_spec = zero_spec
    prev_tap_spec = zero_spec
    grad_block = grad_out
    pieces = []
    for offset in range(segments + 1):
        if offset > 0:
            grad_block = passed_along(grad_block, "ctx", -1)
        is_live = (position + offset < seq_blocks).astype(jnp.float32)
        raw_spec = spectrum(tables, grad_block)
        grad_spec = (raw_spec[0] * is_live, raw_spec[1] * is_live)
        if offset < segments:
            segment_taps = all_taps[:, offset, :]
            tap_spec = spectrum(tables, segment_taps)
        else:
            tap_spec = zero_spec
        kernel_spec = signed_sum(parity, tap_spec, prev_tap_spec)
        added = conj_product(dc_row, kernel_spec, grad_spec)
        input_grad_spec = (input_grad_spec[0] + added[0], input_grad_spec[1] + added[1])
        if offset > 0:
            pair_spec = conj_product(
                dc_row, value_spec, signed_sum(parity, prev_grad_spec, grad_spec)
            )
            pieces.append(reduce_segment(tables, pair_spec))
        prev_grad_spec = grad_spec
        prev_tap_spec = tap_spec
    grad_inputs = inverse(tables, input_grad_spec).astype(jnp.bfloat16)
    grad_stack = jnp.stack(pieces, 1)
    grad_taps = lax.all_to_all(grad_stack, "ch", split_axis=1, concat_axis=2, tiled=True)
    return (grad_inputs, grad_taps)


def solution(mesh):
    placed = (P("ctx", "ch"), P("ctx", "ch"), P("ctx", "ch", None))
    return jax.shard_map(
        shards,
        mesh=mesh,
        in_specs=placed,
        out_specs=(P("ctx", "ch"), P("ctx", "ch", None)),
        check_vma=False,
    )
```

profile of v0, /device:TPU:1, one launch (start us, length us, event | category | flops | bytes accessed | tf_op | source)
XLA Modules:
  0.0 641.0 jit_solution(11371475810876633068)
XLA Ops:
  7.2 2.1 collective-permute-start
  11.6 2.6 fusion.663
  17.4 2.8 fusion.16
  20.8 1.8 convolution_add_fusion
  22.7 2.1 collective-permute-start.1
  26.3 1.6 fusion.673
  29.6 2.0 fusion.14
  32.9 2.3 convolution_add_fusion.43
  35.3 2.3 collective-permute-start.2
  41.1 2.3 convolution_add_fusion.42
  43.5 3.2 collective-permute-done.2
  46.7 1.9 collective-permute-start.3
  52.3 2.3 convolution_add_fusion.41
  54.7 2.5 collective-permute-done.3
  57.2 2.2 collective-permute-start.4
  63.0 2.2 convolution_add_fusion.40
  65.3 3.2 collective-permute-done.4
  68.5 1.9 collective-permute-start.5
  74.0 2.3 convolution_add_fusion.39
  76.4 2.6 collective-permute-done.5
  79.0 2.4 collective-permute-start.6
  85.0 2.3 convolution_add_fusion.38
  87.3 3.2 collective-permute-done.6
  90.6 1.9 collective-permute-start.7
  96.1 2.3 convolution_add_fusion.37
  98.7 2.4 collective-permute-done.7
  104.7 2.3 convolution_add_fusion.36
  107.0 4.6 copy.14
  111.7 6.1 reshape.10
  117.8 7.8 %all_to_all.36 = bf16[2,2,32768]{2,1,0:T(2,128)(2,1)S(1)} all-to-all(bf16[2,2,32768]{2,1,0:T(2,128)(2,1)S(1)} %reshape.10), channel_id=1, replica_groups=mesh['ctx'=16,'ch'=2] {'ch'}, dimensions={0} | all-to-all | bytes 524288 | tf_op jit(solution)/shard_map/all_to_all | solution.py:85
  125.7 6.2 reshape.11
  131.8 6.1 copy.18
  140.2 17.9 %reduce-scatter.11.cloned.1.call-done = f32[8,2048]{1,0:T(8,128)} async-done(((f32[128,2048]{1,0:T(8,128)}), f32[8,2048]{1,0:T(8,128)}) %reduce-scatter.11.cloned.1.call-update) | async-done | bytes 65552 | tf_op jit(solution)/shard_map/reduce_scatter | solution.py:74
  159.6 58.6 %reduce-scatter.13.cloned.1.call-done = f32[8,2048]{1,0:T(8,128)} async-done(((f32[128,2048]{1,0:T(8,128)}), f32[8,2048]{1,0:T(8,128)}) %reduce-scatter.13.cloned.1.call-update) | async-done | bytes 65552 | tf_op jit(solution)/shard_map/reduce_scatter | solution.py:74
  219.6 58.9 %reduce-scatter.15.cloned.1.call-done = f32[8,2048]{1,0:T(8,128)} async-done(((f32[128,2048]{1,0:T(8,128)}), f32[8,2048]{1,0:T(8,128)}) %reduce-scatter.15.cloned.1.call-update) | async-done | bytes 65552 | tf_op jit(solution)/shard_map/reduce_scatter | solution.py:74
  280.1 58.4 %reduce-scatter.17.cloned.1.call-done = f32[8,2048]{1,0:T(8,128)} async-done(((f32[128,2048]{1,0:T(8,128)}), f32[8,2048]{1,0:T(8,128)}) %reduce-scatter.17.cloned.1.call-update) | async-done | bytes 65552 | tf_op jit(solution)/shard_map/reduce_scatter | solution.py:74
  340.0 58.9 %reduce-scatter.19.cloned.1.call-done = f32[8,2048]{1,0:T(8,128)} async-done(((f32[128,2048]{1,0:T(8,128)}), f32[8,2048]{1,0:T(8,128)}) %reduce-scatter.19.cloned.1.call-update) | async-done | bytes 65552 | tf_op jit(solution)/shard_map/reduce_scatter | solution.py:74
  400.3 58.6 %reduce-scatter.21.cloned.1.call-done = f32[8,2048]{1,0:T(8,128)} async-done(((f32[128,2048]{1,0:T(8,128)}), f32[8,2048]{1,0:T(8,128)}) %reduce-scatter.21.cloned.1.call-update) | async-done | bytes 65552 | tf_op jit(solution)/shard_map/reduce_scatter | solution.py:74
  460.4 59.0 %reduce-scatter.23.cloned.1.call-done = f32[8,2048]{1,0:T(8,128)} async-done(((f32[128,2048]{1,0:T(8,128)}), f32[8,2048]{1,0:T(8,128)}) %reduce-scatter.23.cloned.1.call-update) | async-done | bytes 65552 | tf_op jit(solution)/shard_map/reduce_scatter | solution.py:74
  520.8 3.7 all-to-all-start.1
  524.5 5.4 all-to-all-done.1
  531.7 42.4 %all-gather.2.cloned.1.call-done = bf16[128,8,2048]{2,0,1:T(8,128)(2,1)} async-done(((bf16[8,8,2048]{2,0,1:T(8,128)(2,1)}), bf16[128,8,2048]{2,0,1:T(8,128)(2,1)}) %all-gather.2.cloned.1.call-update) | async-done | bytes 4194320 | tf_op jit(solution)/shard_map/all_gather | solution.py:86
  574.0 1.8 fusion.246
  577.4 1.6 fusion.232
  596.1 1.6 convolution_add_fusion.29
  597.8 1.8 convolution_add_fusion.9
  612.4 9.9 %fusion.127 = f32[128,2048]{1,0:T(8,128)} fusion(f32[128,2048]{1,0:T(8,128)S(1)} %copy-done.48, f32[128,2048]{1,0:T(8,128)S(1)} %copy-done.41, f32[128,2048]{1,0:T(8,128)S(1)} %copy-done.35, f32[128,2048]{1,0:T(8,128)S(1)} %copy-done.29, f32[128,2048]{1,0:T(8,128)S(1)} %copy-done.23, f32[128,2048]{1,0:T(8,128)S(1)} %copy-done.17, ...), kind=kOutput, calls=%fused_computation.188 | convolution fusion | flops 221528064 | bytes 36701312 | tf_op jit(solution)/shard_map/dot_general | solution.py:52
  622.3 11.7 %fusion.18 = bf16[128,2048]{1,0:T(8,128)(2,1)} fusion(f32[128,2048]{1,0:T(8,128)} %fusion.127, f32[128,2048]{1,0:T(8,128)S(1)} %copy-done.48, f32[128,2048]{1,0:T(8,128)} %copy-done.51, f32[128,2048]{1,0:T(8,128)S(1)} %copy-done.41, f32[128,2048]{1,0:T(8,128)S(1)} %copy-done.44, f32[128,2048]{1,0:T(8,128)S(1)} %copy-done.35, ...), kind=kOutput, calls=%fused_computation.63 | convolution fusion | flops 224460800 | bytes 37226752 | tf_op jit(solution)/shard_map/dot_general | solution.py:55
  (216 shorter events, 81.5 us)
Async XLA Ops:
  7.2 8.6 %copy-start.52 = (bf16[128,2048]{1,0:T(8,128)(2,1)S(1)}, bf16[128,2048]{1,0:T(8,128)(2,1)}, u32[]{:S(2)}) copy-start(bf16[128,2048]{1,0:T(8,128)(2,1)} %param.3) | copy-start | bytes 1572868
  7.2 131.6 %reduce-scatter.9.cloned.1.call-start = ((), (), s32[]{:S(2)}) async-start(), calls=%async_computation.11 | async-start | bytes 1114112 | tf_op jit(solution)/shard_map/reduce_scatter | solution.py:74
  7.2 15.4 %collective-permute-start = (bf16[128,2048]{1,0:T(8,128)(2,1)}, bf16[128,2048]{1,0:T(8,128)(2,1)}, u32[]{:S(2)}, u32[]{:S(2)}) collective-permute-start(bf16[128,2048]{1,0:T(8,128)(2,1)} %param.3), channel_id=1, source_target_pairs={{2,0},{4,2},{6,4},{8,6},{10,8},{12,10},{14,12},{16,14},{18,16},{20... | collective-permute-start | bytes 1572872 | tf_op jit(solution)/shard_map/ppermute | solution.py:14
  22.6 9.0 %copy-start.45 = (f32[128,2048]{1,0:T(8,128)S(1)}, f32[128,2048]{1,0:T(8,128)}, u32[]{:S(2)}) copy-start(f32[128,2048]{1,0:T(8,128)} %fusion.17) | copy-start | bytes 3145732
  22.6 9.0 %copy-start.49 = (f32[128,2048]{1,0:T(8,128)S(1)}, f32[128,2048]{1,0:T(8,128)}, u32[]{:S(2)}) copy-start(f32[128,2048]{1,0:T(8,128)} %fusion.16) | copy-start | bytes 3145732
  22.7 12.6 %collective-permute-start.1 = (bf16[128,2048]{1,0:T(8,128)(2,1)}, bf16[128,2048]{1,0:T(8,128)(2,1)S(1)}, u32[]{:S(2)}, u32[]{:S(2)}) collective-permute-start(bf16[128,2048]{1,0:T(8,128)(2,1)} %collective-permute-done), channel_id=1, source_target_pairs={{2,0},{4,2},{6,4},{8,6},{10,8},{12,10},{14,12},{16,14},{18,16},{20... | collective-permute-start | bytes 1572872 | tf_op jit(solution)/shard_map/ppermute | solution.py:14
  35.2 123.0 %reduce-scatter.11.cloned.1.call-start = ((), (), s32[]{:S(2)}) async-start(), calls=%async_computation.12 | async-start | bytes 1114112 | tf_op jit(solution)/shard_map/reduce_scatter | solution.py:74
  35.3 11.5 %collective-permute-start.2 = (bf16[128,2048]{1,0:T(8,128)(2,1)S(1)}, bf16[128,2048]{1,0:T(8,128)(2,1)S(1)}, u32[]{:S(2)}, u32[]{:S(2)}) collective-permute-start(bf16[128,2048]{1,0:T(8,128)(2,1)S(1)} %collective-permute-done.1), channel_id=1, source_target_pairs={{2,0},{4,2},{6,4},{8,6},{10,8},{12,10},{14,12},{16,14},{18,16},{20... | collective-permute-start | bytes 1572872 | tf_op jit(solution)/shard_map/ppermute | solution.py:14
  43.4 174.7 %reduce-scatter.13.cloned.1.call-start = ((), (), s32[]{:S(2)}) async-start(), calls=%async_computation.13 | async-start | bytes 1114112 | tf_op jit(solution)/shard_map/reduce_scatter | solution.py:74
  43.5 7.5 %copy-start.10 = (f32[128,2048]{1,0:T(8,128)S(1)}, f32[128,2048]{1,0:T(8,128)}, u32[]{:S(2)}) copy-start(f32[128,2048]{1,0:T(8,128)} %copy-done.9) | copy-start | bytes 3145732
  43.5 7.5 %copy-start.13 = (f32[128,2048]{1,0:T(8,128)S(1)}, f32[128,2048]{1,0:T(8,128)}, u32[]{:S(2)}) copy-start(f32[128,2048]{1,0:T(8,128)} %copy-done.12) | copy-start | bytes 3145732
  46.7 10.5 %collective-permute-start.3 = (bf16[128,2048]{1,0:T(8,128)(2,1)S(1)}, bf16[128,2048]{1,0:T(8,128)(2,1)S(1)}, u32[]{:S(2)}, u32[]{:S(2)}) collective-permute-start(bf16[128,2048]{1,0:T(8,128)(2,1)S(1)} %collective-permute-done.2), channel_id=1, source_target_pairs={{2,0},{4,2},{6,4},{8,6},{10,8},{12,10},{14,12},{16,14},{18,16},{20... | collective-permute-start | bytes 1572872 | tf_op jit(solution)/shard_map/ppermute | solution.py:14
  54.6 224.0 %reduce-scatter.15.cloned.1.call-start = ((), (), s32[]{:S(2)}) async-start(), calls=%async_computation.14 | async-start | bytes 1114112 | tf_op jit(solution)/shard_map/reduce_scatter | solution.py:74
  54.7 7.1 %copy-start.16 = (f32[128,2048]{1,0:T(8,128)S(1)}, f32[128,2048]{1,0:T(8,128)}, u32[]{:S(2)}) copy-start(f32[128,2048]{1,0:T(8,128)} %copy-done.15) | copy-start | bytes 3145732
  54.7 7.1 %copy-start.19 = (f32[128,2048]{1,0:T(8,128)S(1)}, f32[128,2048]{1,0:T(8,128)}, u32[]{:S(2)}) copy-start(f32[128,2048]{1,0:T(8,128)} %copy-done.18) | copy-start | bytes 3145732
  57.2 11.3 %collective-permute-start.4 = (bf16[128,2048]{1,0:T(8,128)(2,1)S(1)}, bf16[128,2048]{1,0:T(8,128)(2,1)S(1)}, u32[]{:S(2)}, u32[]{:S(2)}) collective-permute-start(bf16[128,2048]{1,0:T(8,128)(2,1)S(1)} %collective-permute-done.3), channel_id=1, source_target_pairs={{2,0},{4,2},{6,4},{8,6},{10,8},{12,10},{14,12},{16,14},{18,16},{20... | collective-permute-start | bytes 1572872 | tf_op jit(solution)/shard_map/ppermute | solution.py:14
  65.3 273.2 %reduce-scatter.17.cloned.1.call-start = ((), (), s32[]{:S(2)}) async-start(), calls=%async_computation.15 | async-start | bytes 1114112 | tf_op jit(solution)/shard_map/reduce_scatter | solution.py:74
  65.3 7.5 %copy-start.22 = (f32[128,2048]{1,0:T(8,128)S(1)}, f32[128,2048]{1,0:T(8,128)}, u32[]{:S(2)}) copy-start(f32[128,2048]{1,0:T(8,128)} %copy-done.21) | copy-start | bytes 3145732
  65.3 7.5 %copy-start.25 = (f32[128,2048]{1,0:T(8,128)S(1)}, f32[128,2048]{1,0:T(8,128)}, u32[]{:S(2)}) copy-start(f32[128,2048]{1,0:T(8,128)} %copy-done.24) | copy-start | bytes 3145732
  68.5 10.5 %collective-permute-start.5 = (bf16[128,2048]{1,0:T(8,128)(2,1)S(1)}, bf16[128,2048]{1,0:T(8,128)(2,1)S(1)}, u32[]{:S(2)}, u32[]{:S(2)}) collective-permute-start(bf16[128,2048]{1,0:T(8,128)(2,1)S(1)} %collective-permute-done.4), channel_id=1, source_target_pairs={{2,0},{4,2},{6,4},{8,6},{10,8},{12,10},{14,12},{16,14},{18,16},{20... | collective-permute-start | bytes 1572872 | tf_op jit(solution)/shard_map/ppermute | solution.py:14
  76.3 322.5 %reduce-scatter.19.cloned.1.call-start = ((), (), s32[]{:S(2)}) async-start(), calls=%async_computation.16 | async-start | bytes 1114112 | tf_op jit(solution)/shard_map/reduce_scatter | solution.py:74
  76.3 7.4 %copy-start.28 = (f32[128,2048]{1,0:T(8,128)S(1)}, f32[128,2048]{1,0:T(8,128)}, u32[]{:S(2)}) copy-start(f32[128,2048]{1,0:T(8,128)} %copy-done.27) | copy-start | bytes 3145732
  76.4 7.4 %copy-start.31 = (f32[128,2048]{1,0:T(8,128)S(1)}, f32[128,2048]{1,0:T(8,128)}, u32[]{:S(2)}) copy-start(f32[128,2048]{1,0:T(8,128)} %copy-done.30) | copy-start | bytes 3145732
  79.0 11.6 %collective-permute-start.6 = (bf16[128,2048]{1,0:T(8,128)(2,1)S(1)}, bf16[128,2048]{1,0:T(8,128)(2,1)S(1)}, u32[]{:S(2)}, u32[]{:S(2)}) collective-permute-start(bf16[128,2048]{1,0:T(8,128)(2,1)S(1)} %collective-permute-done.5), channel_id=1, source_target_pairs={{2,0},{4,2},{6,4},{8,6},{10,8},{12,10},{14,12},{16,14},{18,16},{20... | collective-permute-start | bytes 1572872 | tf_op jit(solution)/shard_map/ppermute | solution.py:14
  87.3 371.6 %reduce-scatter.21.cloned.1.call-start = ((), (), s32[]{:S(2)}) async-start(), calls=%async_computation.17 | async-start | bytes 1114112 | tf_op jit(solution)/shard_map/reduce_scatter | solution.py:74
  87.3 7.5 %copy-start.34 = (f32[128,2048]{1,0:T(8,128)S(1)}, f32[128,2048]{1,0:T(8,128)}, u32[]{:S(2)}) copy-start(f32[128,2048]{1,0:T(8,128)} %copy-done.33) | copy-start | bytes 3145732
  87.3 7.5 %copy-start.37 = (f32[128,2048]{1,0:T(8,128)S(1)}, f32[128,2048]{1,0:T(8,128)}, u32[]{:S(2)}) copy-start(f32[128,2048]{1,0:T(8,128)} %copy-done.36) | copy-start | bytes 3145732
  90.6 10.5 %collective-permute-start.7 = (bf16[128,2048]{1,0:T(8,128)(2,1)S(1)}, bf16[128,2048]{1,0:T(8,128)(2,1)S(1)}, u32[]{:S(2)}, u32[]{:S(2)}) collective-permute-start(bf16[128,2048]{1,0:T(8,128)(2,1)S(1)} %collective-permute-done.6), channel_id=1, source_target_pairs={{2,0},{4,2},{6,4},{8,6},{10,8},{12,10},{14,12},{16,14},{18,16},{20... | collective-permute-start | bytes 1572872 | tf_op jit(solution)/shard_map/ppermute | solution.py:14
  98.4 420.9 %reduce-scatter.23.cloned.1.call-start = ((), (), s32[]{:S(2)}) async-start(), calls=%async_computation.18 | async-start | bytes 1114112 | tf_op jit(solution)/shard_map/reduce_scatter | solution.py:74
  107.0 467.1 %all-gather.2.cloned.1.call-start = ((), (), s32[]{:S(2)}) async-start(), calls=%async_computation.10 | async-start | bytes 4456448 | tf_op jit(solution)/shard_map/all_gather | solution.py:86
  520.8 9.1 %all-to-all-start.1 = ((f32[8,8,2048]{2,0,1:T(8,128)}), f32[8,8,2048]{2,0,1:T(8,128)S(1)}, u32[]{:S(2)}, u32[]{:S(2)}) async-start(f32[8,8,2048]{2,0,1:T(8,128)} %bitcast_dynamic-update-slice_fusion), calls=%async_computation.9 | async-start | bytes 1048576 | tf_op jit(solution)/shard_map/all_to_all | solution.py:121
  574.0 5.0 copy-start.2
  599.6 12.7 %copy-start.50 = (f32[128,2048]{1,0:T(8,128)S(1)}, f32[128,2048]{1,0:T(8,128)}, u32[]{:S(2)}) copy-start(f32[128,2048]{1,0:T(8,128)} %fusion.16) | copy-start | bytes 3145732
  601.1 11.1 %copy-start.48 = (f32[128,2048]{1,0:T(8,128)S(1)}, f32[128,2048]{1,0:T(8,128)}, u32[]{:S(2)}) copy-start(f32[128,2048]{1,0:T(8,128)} %copy-done.47) | copy-start | bytes 3145732
  602.7 9.6 %copy-start.41 = (f32[128,2048]{1,0:T(8,128)S(1)}, f32[128,2048]{1,0:T(8,128)}, u32[]{:S(2)}) copy-start(f32[128,2048]{1,0:T(8,128)} %copy-done.39) | copy-start | bytes 3145732
  602.7 9.6 %copy-start.44 = (f32[128,2048]{1,0:T(8,128)S(1)}, f32[128,2048]{1,0:T(8,128)}, u32[]{:S(2)}) copy-start(f32[128,2048]{1,0:T(8,128)} %copy-done.42) | copy-start | bytes 3145732
  602.7 9.6 %copy-start.46 = (f32[128,2048]{1,0:T(8,128)S(1)}, f32[128,2048]{1,0:T(8,128)}, u32[]{:S(2)}) copy-start(f32[128,2048]{1,0:T(8,128)} %fusion.17) | copy-start | bytes 3145732
  604.3 8.0 %copy-start.35 = (f32[128,2048]{1,0:T(8,128)S(1)}, f32[128,2048]{1,0:T(8,128)}, u32[]{:S(2)}) copy-start(f32[128,2048]{1,0:T(8,128)} %copy-done.33) | copy-start | bytes 3145732
  604.3 8.0 %copy-start.38 = (f32[128,2048]{1,0:T(8,128)S(1)}, f32[128,2048]{1,0:T(8,128)}, u32[]{:S(2)}) copy-start(f32[128,2048]{1,0:T(8,128)} %copy-done.36) | copy-start | bytes 3145732
  605.9 6.4 %copy-start.26 = (f32[128,2048]{1,0:T(8,128)S(1)}, f32[128,2048]{1,0:T(8,128)}, u32[]{:S(2)}) copy-start(f32[128,2048]{1,0:T(8,128)} %copy-done.24) | copy-start | bytes 3145732
  605.9 6.4 %copy-start.29 = (f32[128,2048]{1,0:T(8,128)S(1)}, f32[128,2048]{1,0:T(8,128)}, u32[]{:S(2)}) copy-start(f32[128,2048]{1,0:T(8,128)} %copy-done.27) | copy-start | bytes 3145732
  605.9 6.5 %copy-start.32 = (f32[128,2048]{1,0:T(8,128)S(1)}, f32[128,2048]{1,0:T(8,128)}, u32[]{:S(2)}) copy-start(f32[128,2048]{1,0:T(8,128)} %copy-done.30) | copy-start | bytes 3145732
  607.5 4.9 copy-start.11
  607.5 4.9 copy-start.14
  607.5 4.9 copy-start.17
  607.5 4.9 copy-start.20
  607.5 4.9 copy-start.23
  622.3 11.7 %copy-start.1 = (bf16[128,2048]{1,0:T(8,128)(2,1)S(1)}, bf16[128,2048]{1,0:T(8,128)(2,1)}, u32[]{:S(2)}) copy-start(bf16[128,2048]{1,0:T(8,128)(2,1)} %param.4) | copy-start | bytes 1572868
  (24 other events, 60.6 us)
Sparse Core Ops, SparseCore 0:
  35.3 62.4 reduce-scatter.8
  101.8 56.2 reduce-scatter.10
  161.8 56.3 reduce-scatter.12
  222.1 56.4 reduce-scatter.14
  282.1 56.3 reduce-scatter.16
  342.4 56.3 reduce-scatter.18
  402.4 56.3 reduce-scatter.20
  462.9 56.3 reduce-scatter.22
  522.1 51.8 all-gather.1
where the time goes:
time: 649 us; the launch traced here: 641 us
  waiting for transfers between devices  435 us (67%)
  matrix products  124 us (19%)
  local copies, waits for them, and re-layouts  37.6 us (6%)
  starting transfers between devices  20.9 us (3%)
  between operations  15.5 us (2%)
  blocking collectives  7.83 us (1%)
    reduce_scatter x8, waiting for transfers between devices, reduce_segment(): lax.psum_scatter(inverse(tables, spec), 'ctx', scatter_dimension=0, tiled...  370 us
    dot_general x36, matrix products, split_dot(): return first + jnp.dot(pair[1], signal, preferred_element_type=jnp.float32)  43.7 us
    all_gather x1, waiting for transfers between devices, shards(): all_taps = lax.all_gather(own_taps, 'ctx', axis=0, tiled=True)  42.4 us
    dot_general x36, matrix products, split_dot(): first = jnp.dot(pair[0], signal, preferred_element_type=jnp.float32)  30.8 us
    dot_general x9, matrix products, inverse(): jnp.dot(tables[3], spec[1], precision=HIGH_PREC, preferred_element_type=j...  29.9 us
    unnamed x118, local copies, waits for them, and re-layouts  27.5 us
    dot_general x9, matrix products, inverse(): jnp.dot(tables[2], spec[0], precision=HIGH_PREC, preferred_element_type=j...  19.4 us
    ppermute x8, waiting for transfers between devices, passed_along(): return lax.ppermute(block, axis, route)  17.2 us
  transfers between devices with their start and end apart: 18, of which 15 were waited for; matrix products, arithmetic and copies ran while one was open for 16% of the time, Pallas kernels for 0%

commit v1 on v0

v1 whole, which is shorter than its diff:
```python
import functools

import jax
import jax.numpy as jnp
import numpy as np
from jax import lax
from jax.experimental import pallas as pl
from jax.experimental.pallas import tpu as pltpu
from jax.sharding import PartitionSpec as P

F32 = jnp.float32
BF16 = jnp.bfloat16


def two_bf16(table):
    upper = table.astype(np.float32).astype(jnp.bfloat16)
    lower = (table - upper.astype(np.float64)).astype(np.float32).astype(jnp.bfloat16)
    return upper, lower


def dft_tables(block):
    freq = np.concatenate([np.arange(0, block, 2), np.arange(1, block, 2)])
    turns = ((2 * freq[:, None] + 1) * np.arange(block)[None, :]) % (4 * block)
    angle = turns * (np.pi / (2 * block))
    forward = np.concatenate([np.cos(angle), -np.sin(angle)], 0)
    return two_bf16(forward) + two_bf16(forward.T / block)


def forward_dft(tables, block, columns):
    upper, lower = tables
    first = jnp.dot(upper[...], columns, preferred_element_type=F32)
    return first + jnp.dot(lower[...], columns, preferred_element_type=F32)


def inverse_dft(tables, spec):
    upper, lower = tables
    head = spec.astype(BF16)
    tail = (spec - head.astype(F32)).astype(BF16)
    total = jnp.dot(upper[...], head, preferred_element_type=F32)
    total += jnp.dot(lower[...], head, preferred_element_type=F32)
    return total + jnp.dot(upper[...], tail, preferred_element_type=F32)


def side_by_side(width):
    return 2 if width % 128 == 0 else 1


def spectra(tables, block, rows_ref, spec_ref):
    count, _, width = spec_ref.shape
    group = side_by_side(width)
    for j in range(0, count, group):
        parts = [rows_ref[pl.ds((j + u) * block, block), :] for u in range(group)]
        both = forward_dft(tables, block, jnp.concatenate(parts, 1) if group > 1 else parts[0])
        for u in range(group):
            spec_ref[j + u] = both[:, u * width : (u + 1) * width]


def windows(block, spec_ref, window_ref):
    count = spec_ref.shape[0]
    half = block // 2
    for j in range(count):
        if j + 1 == count:
            window_ref[j] = spec_ref[j]
            continue
        for start, sign in ((0, 1), (half, -1)):
            real, imag = pl.ds(start, half), pl.ds(block + start, half)
            next_imag, next_real = spec_ref[j + 1, imag], spec_ref[j + 1, real]
            if sign > 0:
                window_ref[j, real] = spec_ref[j, real] + next_imag
                window_ref[j, imag] = spec_ref[j, imag] - next_real
            else:
                window_ref[j, real] = spec_ref[j, real] - next_imag
                window_ref[j, imag] = spec_ref[j, imag] + next_real


def correlate(block, left_ref, window_ref, out_ref):
    lefts, outs, count = left_ref.shape[0], out_ref.shape[0], window_ref.shape[0]

    def body(t, carry):
        real = pl.ds(pl.multiple_of(t * 8, 8), 8)
        imag = pl.ds(pl.multiple_of(block + t * 8, 8), 8)
        for a in range(outs):
            sum_real = sum_imag = None
            for s in range(min(lefts, count - a)):
                lr, li = left_ref[s, real], left_ref[s, imag]
                wr, wi = window_ref[a + s, real], window_ref[a + s, imag]
                re = lr * wr + li * wi
                im = lr * wi - li * wr
                sum_real = re if sum_real is None else sum_real + re
                sum_imag = im if sum_imag is None else sum_imag + im
            out_ref[a, real] = sum_real
            out_ref[a, imag] = sum_imag
        return carry

    lax.fori_loop(0, block // 8, body, 0)


def invert(tables, block, spec_ref, out_ref):
    count, _, width = spec_ref.shape
    group = side_by_side(width)
    for j in range(0, count, group):
        parts = [spec_ref[j + u] for u in range(group)]
        both = inverse_dft(tables, jnp.concatenate(parts, 1) if group > 1 else parts[0])
        for u in range(group):
            out_ref[pl.ds((j + u) * block, block), :] = both[
                :, u * width : (u + 1) * width
            ].astype(out_ref.dtype)


def input_grad_kernel(block, grad_ref, taps_ref, fu, fl, iu, il, out_ref, window_ref, spec, tap_spec):
    spectra((fu, fl), block, grad_ref, spec)
    windows(block, spec, window_ref)
    spectra((fu, fl), block, taps_ref, tap_spec)
    correlate(block, tap_spec, window_ref, spec)
    invert((iu, il), block, spec, out_ref)


def tap_grad_kernel(block, value_ref, window_ref, fu, fl, iu, il, out_ref, spec, tap_spec):
    spectra((fu, fl), block, value_ref, spec)
    correlate(block, spec, window_ref, tap_spec)
    invert((iu, il), block, tap_spec, out_ref)


def call_kernel(body, out_shape, scratch, operands, flops):
    padded = sum(
        int(np.prod(a.shape[:-1])) * max(a.shape[-1], 128) * 4
        for a in list(operands) + list(out_shape) + list(scratch)
    )
    moved = sum(int(np.prod(a.shape)) * a.dtype.itemsize for a in list(operands) + list(out_shape))
    return pl.pallas_call(
        body,
        out_shape=out_shape,
        in_specs=[pl.BlockSpec(memory_space=pltpu.VMEM)] * len(operands),
        out_specs=[pl.BlockSpec(memory_space=pltpu.VMEM)] * len(out_shape),
        scratch_shapes=[pltpu.VMEM(a.shape, a.dtype) for a in scratch],
        compiler_params=pltpu.CompilerParams(vmem_limit_bytes=min(padded + (8 << 20), 56 << 20)),
        cost_estimate=pl.CostEstimate(flops=flops, bytes_accessed=moved, transcendentals=0),
    )(*operands)


def shards(grad_out, inputs, filter_taps):
    rows, width = grad_out.shape
    ctx, ch = lax.axis_size("ctx"), lax.axis_size("ch")
    tap_rows, tap_segs, channels = filter_taps.shape
    own = width // ctx
    block = 2 * rows
    length = rows * ctx
    taps = rows * tap_segs * ch
    shape = jax.ShapeDtypeStruct

    def to_channels(array):
        parts = array.reshape(rows, ctx, own).transpose(1, 0, 2)
        return lax.all_to_all(parts, "ctx", 0, 0, tiled=True).reshape(length, own)

    grad = to_channels(grad_out)
    tap_parts = filter_taps.reshape(tap_rows, tap_segs, ch, ctx, own).transpose(3, 2, 0, 1, 4)
    tap_parts = tap_parts.reshape(ctx * ch, tap_rows, tap_segs, own)
    tap_parts = lax.all_to_all(tap_parts, ("ctx", "ch"), 0, 0, tiled=True)
    tap_all = tap_parts.reshape(ctx, ch, tap_rows, tap_segs, own).transpose(1, 3, 0, 2, 4)
    tap_all = tap_all.reshape(taps, own)
    value = to_channels(inputs)

    tables = tuple(jnp.asarray(t) for t in dft_tables(block))
    blocks, tap_blocks = length // block, taps // block
    spec = shape((blocks, 2 * block, own), F32)
    tap_spec = shape((tap_blocks, 2 * block, own), F32)
    flops = 2 * 2 * block * block * own * (blocks * 5 + tap_blocks * 2)
    input_grad, window = call_kernel(
        functools.partial(input_grad_kernel, block),
        [shape((length, own), BF16), spec],
        [spec, tap_spec],
        (grad, tap_all) + tables,
        flops,
    )
    (tap_grad,) = call_kernel(
        functools.partial(tap_grad_kernel, block),
        [shape((taps, own), BF16)],
        [spec, tap_spec],
        (value, window) + tables,
        flops,
    )

    back = lax.all_to_all(input_grad.reshape(ctx, rows, own), "ctx", 0, 0, tiled=True)
    grad_inputs = back.transpose(1, 0, 2).reshape(rows, width)
    out_parts = tap_grad.reshape(ch, tap_segs, ctx, tap_rows, own).transpose(2, 0, 3, 1, 4)
    out_parts = out_parts.reshape(ctx * ch, tap_rows, tap_segs, own)
    out_parts = lax.all_to_all(out_parts, ("ctx", "ch"), 0, 0, tiled=True)
    out_parts = out_parts.reshape(ctx, ch, tap_rows, tap_segs, own).transpose(2, 3, 1, 0, 4)
    grad_taps = out_parts.reshape(tap_rows, tap_segs, channels).astype(F32)
    return grad_inputs, grad_taps


def solution(mesh):
    return jax.shard_map(
        shards,
        mesh=mesh,
        in_specs=(P("ctx", "ch"), P("ctx", "ch"), P("ctx", "ch", None)),
        out_specs=(P("ctx", "ch"), P("ctx", "ch", None)),
        check_vma=False,
    )
```

time: 649 us -> 94.8 us (0.15); the launches traced: 641 us -> 93.8 us
  waiting for transfers between devices: 435 us -> 44.4 us
  matrix products: 124 us -> 0 us
  local copies, waits for them, and re-layouts: 37.6 us -> 9.28 us
  between operations: 15.5 us -> 0.75 us
    reduce_scatter x8 -> x0, waiting for transfers between devices: 370 us -> none  [reduce_segment(): lax.psum_scatter(inverse(tables, spec), 'ctx', scatter_dimension=0, tiled...]
    dot_general x90 -> x0, matrix products: 124 us -> none  [the longest x36 43.7 us: split_dot(): return first + jnp.dot(pair[1], signal, preferred_element_type=jnp.float32)]
    all_gather x1 -> x0, waiting for transfers between devices: 42.4 us -> none  [shards(): all_taps = lax.all_gather(own_taps, 'ctx', axis=0, tiled=True)]
    all_to_all x1 -> x4, waiting for transfers between devices: 5.38 us -> 44.4 us  [the longest x2 22 us: to_channels(): return lax.all_to_all(parts, 'ctx', 0, 0, tiled=True).reshape(length, own)]
    unnamed x118 -> x18, local copies, waits for them, and re-layouts: 27.5 us -> 4.23 us
    ppermute x8 -> x0, waiting for transfers between devices: 17.2 us -> none  [passed_along(): return lax.ppermute(block, axis, route)]
    ppermute x8 -> x0, starting transfers between devices: 16.7 us -> none  [passed_along(): return lax.ppermute(block, axis, route)]
    all_to_all x1 -> x4, starting transfers between devices: 3.7 us -> 19 us  [the longest x2 8.19 us: to_channels(): return lax.all_to_all(parts, 'ctx', 0, 0, tiled=True).reshape(length, own)]
  transfers between devices with their start and end apart: 18 -> 4, of which waited for: 15 -> 4; matrix products, arithmetic and copies ran while one was open for 16% -> 3% of each run, Pallas kernels for 0% -> 4%
where the time goes in v1:
time: 94.8 us; the launch traced here: 93.8 us
  waiting for transfers between devices  44.4 us (47%)
  starting transfers between devices  19 us (20%)
  blocking collectives  13.9 us (15%)
  local copies, waits for them, and re-layouts  9.28 us (10%)
  Pallas kernels  6.41 us (7%)
    all_to_all x2, waiting for transfers between devices, to_channels(): return lax.all_to_all(parts, 'ctx', 0, 0, tiled=True).reshape(length, own)  22 us
    all_to_all x1, blocking collectives, shards(): out_parts = lax.all_to_all(out_parts, ('ctx', 'ch'), 0, 0, tiled=True)  13.9 us
    all_to_all x1, waiting for transfers between devices, shards(): lax.all_to_all(input_grad.reshape(ctx, rows, own), 'ctx', 0, 0, tiled=True)  12.8 us
    all_to_all x1, waiting for transfers between devices, shards(): tap_parts = lax.all_to_all(tap_parts, ('ctx', 'ch'), 0, 0, tiled=True)  9.6 us
    all_to_all x2, starting transfers between devices, to_channels(): return lax.all_to_all(parts, 'ctx', 0, 0, tiled=True).reshape(length, own)  8.19 us
    all_to_all x1, starting transfers between devices, shards(): tap_parts = lax.all_to_all(tap_parts, ('ctx', 'ch'), 0, 0, tiled=True)  7.1 us
    pallas_call x2, Pallas kernels, call_kernel(): pl.pallas_call(body, out_shape=out_shape, in_specs=[pl.BlockSpec(memory_s...  6.41 us
    unnamed x18, local copies, waits for them, and re-layouts  4.23 us
  transfers between devices with their start and end apart: 4, of which 4 were waited for; matrix products, arithmetic and copies ran while one was open for 3% of the time, Pallas kernels for 4%

profile of v1, /device:TPU:1, one launch (start us, length us, event | category | flops | bytes accessed | tf_op | source)
XLA Modules:
  0.0 93.8 jit_solution(18354866112974431315)
XLA Ops:
  0.6 0.0 copy-start
  0.6 0.0 copy-start.7
  0.7 1.3 %reshape.60 = bf16[8,4,2,16,128]{4,3,2,1,0:T(8,128)(2,1)S(1)} reshape(bf16[8,4,4096]{2,1,0:T(4,128)(2,1)} %param.9) | data formatting | bytes 524288 | tf_op jit(solution)/shard_map/reshape | solution.py:156
  2.0 0.9 copy.19
  2.9 7.1 %all-to-all-start.1 = ((bf16[32,8,4,128]{3,1,2,0:T(8,128)(2,1)}), bf16[32,8,4,128]{3,1,2,0:T(8,128)(2,1)S(1)}, u32[]{:S(2)}, u32[]{:S(2)}) async-start(bf16[32,8,4,128]{3,1,2,0:T(8,128)(2,1)} %bitcast.4), calls=%async_computation.1 | async-start | bytes 524288 | tf_op jit(solution)/shard_map/all_to_all | solution.py:158
  10.0 0.0 copy-done
  10.0 0.9 bitcast_bitcast_fusion.1
  10.9 0.0 copy-start.1
  10.9 0.0 copy-start.2
  10.9 0.0 copy-start.3
  10.9 0.0 copy-start.4
  10.9 9.6 %all-to-all-done.1 = bf16[32,8,4,128]{3,1,2,0:T(8,128)(2,1)S(1)} async-done(((bf16[32,8,4,128]{3,1,2,0:T(8,128)(2,1)}), bf16[32,8,4,128]{3,1,2,0:T(8,128)(2,1)S(1)}, u32[]{:S(2)}, u32[]{:S(2)}) %all-to-all-start.1) | async-done | bytes 262176 | tf_op jit(solution)/shard_map/all_to_all | solution.py:158
  20.5 3.8 %all-to-all-start = ((bf16[16,128,128]{2,1,0:T(8,128)(2,1)}), bf16[16,128,128]{2,1,0:T(8,128)(2,1)S(1)}, u32[]{:S(2)}, u32[]{:S(2)}) async-start(bf16[16,128,128]{2,1,0:T(8,128)(2,1)} %bitcast_bitcast_fusion.1), calls=%async_computation | async-start | bytes 1048576 | tf_op jit(solution)/shard_map/all_to_all | solution.py:153
  24.3 0.0 copy-done.7
  24.3 1.0 %bitcast_bitcast_fusion = bf16[16,128,128]{2,1,0:T(8,128)(2,1)} fusion(bf16[128,2048]{1,0:T(8,128)(2,1)S(1)} %copy-done.7), kind=kLoop, calls=%fused_computation.1 | loop fusion | bytes 1048576 | tf_op jit(solution)/shard_map/transpose | solution.py:152
  25.2 13.2 %all-to-all-done = bf16[16,128,128]{2,1,0:T(8,128)(2,1)S(1)} async-done(((bf16[16,128,128]{2,1,0:T(8,128)(2,1)}), bf16[16,128,128]{2,1,0:T(8,128)(2,1)S(1)}, u32[]{:S(2)}, u32[]{:S(2)}) %all-to-all-start) | async-done | bytes 524320 | tf_op jit(solution)/shard_map/all_to_all | solution.py:153
  38.4 4.4 %all-to-all-start.3 = ((bf16[16,128,128]{2,1,0:T(8,128)(2,1)}), bf16[16,128,128]{2,1,0:T(8,128)(2,1)S(1)}, u32[]{:S(2)}, u32[]{:S(2)}) async-start(bf16[16,128,128]{2,1,0:T(8,128)(2,1)} %bitcast_bitcast_fusion), calls=%async_computation.3 | async-start | bytes 1048576 | tf_op jit(solution)/shard_map/all_to_all | solution.py:153
  42.9 0.0 copy-done.1
  42.9 0.0 copy-done.2
  42.9 0.0 copy-done.3
  42.9 0.0 copy-done.4
  42.9 3.9 %shard_map.86 = (bf16[2048,128]{1,0:T(8,128)(2,1)}, f32[8,512,128]{2,1,0:T(8,128)S(1)}) custom-call(bf16[2048,128]{1,0:T(8,128)(2,1)S(1)} %bitcast.41, bf16[1024,128]{1,0:T(8,128)(2,1)S(1)} %bitcast.43, bf16[512,256]{1,0:T(8,128)(2,1)S(1)} %copy-done.3, bf16[512,256]{1,0:T(8,128)(2,1)S(1)} %copy-done.4, bf16[256,512]{1,0:T(8,128)(2,1)S(1)} %copy-done.1, ...), custom_call_target="tpu_custom_call" | custom-call | flops 1610612736 | bytes 4456448 | tf_op jit(solution)/shard_map/pallas_call | solution.py:130
  46.8 0.0 copy-start.5
  46.8 1.3 %copy-done.5 = f32[8,512,128]{2,1,0:T(8,128)} copy-done((f32[8,512,128]{2,1,0:T(8,128)}, f32[8,512,128]{2,1,0:T(8,128)S(1)}, u32[]{:S(2)}) %copy-start.5) | copy-done | bytes 2097176
  48.1 8.8 %all-to-all-done.3 = bf16[16,128,128]{2,1,0:T(8,128)(2,1)S(1)} async-done(((bf16[16,128,128]{2,1,0:T(8,128)(2,1)}), bf16[16,128,128]{2,1,0:T(8,128)(2,1)S(1)}, u32[]{:S(2)}, u32[]{:S(2)}) %all-to-all-start.3) | async-done | bytes 524320 | tf_op jit(solution)/shard_map/all_to_all | solution.py:153
  56.9 0.0 copy-start.6
  56.9 1.6 %copy-done.6 = f32[8,512,128]{2,1,0:T(8,128)S(1)} copy-done((f32[8,512,128]{2,1,0:T(8,128)S(1)}, f32[8,512,128]{2,1,0:T(8,128)}, u32[]{:S(2)}) %copy-start.6) | copy-done | bytes 2097176
  58.5 2.5 %shard_map.87 = bf16[1024,128]{1,0:T(8,128)(2,1)S(1)} custom-call(bf16[2048,128]{1,0:T(8,128)(2,1)S(1)} %bitcast.40, f32[8,512,128]{2,1,0:T(8,128)S(1)} %copy-done.6, bf16[512,256]{1,0:T(8,128)(2,1)S(1)} %copy-done.3, bf16[512,256]{1,0:T(8,128)(2,1)S(1)} %copy-done.4, bf16[256,512]{1,0:T(8,128)(2,1)S(1)} %copy-done.1, bf16[256,512]{1,0:T(8,128)(2,1)S(1)} %copy-done.2), custom_call_target="tpu_custom_call" | custom-call | flops 1610612736 | bytes 3932160 | tf_op jit(solution)/shard_map/pallas_call | solution.py:130
  61.0 0.1 copy.23
  61.1 13.9 %all_to_all.25 = bf16[32,8,4,128]{3,1,2,0:T(8,128)(2,1)S(1)} all-to-all(bf16[32,8,4,128]{3,1,2,0:T(8,128)(2,1)S(1)} %bitcast.46), channel_id=1, replica_groups=mesh['ctx'=16,'ch'=2] {'ctx','ch'}, dimensions={0} | all-to-all | bytes 524288 | tf_op jit(solution)/shard_map/all_to_all | solution.py:187
  75.0 3.8 %all-to-all-start.2 = ((bf16[16,128,128]{2,1,0:T(8,128)(2,1)}), bf16[16,128,128]{2,1,0:T(8,128)(2,1)S(1)}, u32[]{:S(2)}, u32[]{:S(2)}) async-start(bf16[16,128,128]{2,1,0:T(8,128)(2,1)} %bitcast.8), calls=%async_computation.2 | async-start | bytes 1048576 | tf_op jit(solution)/shard_map/all_to_all | solution.py:183
  78.8 0.3 copy.28
  79.2 1.0 %reshape.61 = f32[8,4,4096]{2,1,0:T(4,128)} reshape(f32[8,4,2,16,128]{4,3,2,1,0:T(8,128)S(1)} %copy.28) | data formatting | bytes 1048576
  80.1 12.8 %all-to-all-done.2 = bf16[16,128,128]{2,1,0:T(8,128)(2,1)S(1)} async-done(((bf16[16,128,128]{2,1,0:T(8,128)(2,1)}), bf16[16,128,128]{2,1,0:T(8,128)(2,1)S(1)}, u32[]{:S(2)}, u32[]{:S(2)}) %all-to-all-start.2) | async-done | bytes 524320 | tf_op jit(solution)/shard_map/all_to_all | solution.py:183
  92.9 0.9 copy_bitcast_fusion
  (2 shorter events, 0.1 us)
Async XLA Ops:
  0.6 9.3 %copy-start = (bf16[128,2048]{1,0:T(8,128)(2,1)S(1)}, bf16[128,2048]{1,0:T(8,128)(2,1)}, u32[]{:S(2)}) copy-start(bf16[128,2048]{1,0:T(8,128)(2,1)} %param.7) | copy-start | bytes 1572868
  0.6 23.6 %copy-start.7 = (bf16[128,2048]{1,0:T(8,128)(2,1)S(1)}, bf16[128,2048]{1,0:T(8,128)(2,1)}, u32[]{:S(2)}) copy-start(bf16[128,2048]{1,0:T(8,128)(2,1)} %param.8) | copy-start | bytes 1572868
  2.9 17.7 %all-to-all-start.1 = ((bf16[32,8,4,128]{3,1,2,0:T(8,128)(2,1)}), bf16[32,8,4,128]{3,1,2,0:T(8,128)(2,1)S(1)}, u32[]{:S(2)}, u32[]{:S(2)}) async-start(bf16[32,8,4,128]{3,1,2,0:T(8,128)(2,1)} %bitcast.4), calls=%async_computation.1 | async-start | bytes 524288 | tf_op jit(solution)/shard_map/all_to_all | solution.py:158
  10.9 32.0 %copy-start.1 = (bf16[256,512]{1,0:T(8,128)(2,1)S(1)}, bf16[256,512]{1,0:T(8,128)(2,1)}, u32[]{:S(2)}) copy-start(bf16[256,512]{1,0:T(8,128)(2,1)} %constant.10.clone.iu) | copy-start | bytes 786436
  10.9 32.0 %copy-start.2 = (bf16[256,512]{1,0:T(8,128)(2,1)S(1)}, bf16[256,512]{1,0:T(8,128)(2,1)}, u32[]{:S(2)}) copy-start(bf16[256,512]{1,0:T(8,128)(2,1)} %constant.11.clone.il) | copy-start | bytes 786436
  10.9 32.0 %copy-start.3 = (bf16[512,256]{1,0:T(8,128)(2,1)S(1)}, bf16[512,256]{1,0:T(8,128)(2,1)}, u32[]{:S(2)}) copy-start(bf16[512,256]{1,0:T(8,128)(2,1)} %constant.8.clone.fu) | copy-start | bytes 786436
  10.9 32.0 %copy-start.4 = (bf16[512,256]{1,0:T(8,128)(2,1)S(1)}, bf16[512,256]{1,0:T(8,128)(2,1)}, u32[]{:S(2)}) copy-start(bf16[512,256]{1,0:T(8,128)(2,1)} %constant.9.clone.fl) | copy-start | bytes 786436
  20.5 17.9 %all-to-all-start = ((bf16[16,128,128]{2,1,0:T(8,128)(2,1)}), bf16[16,128,128]{2,1,0:T(8,128)(2,1)S(1)}, u32[]{:S(2)}, u32[]{:S(2)}) async-start(bf16[16,128,128]{2,1,0:T(8,128)(2,1)} %bitcast_bitcast_fusion.1), calls=%async_computation | async-start | bytes 1048576 | tf_op jit(solution)/shard_map/all_to_all | solution.py:153
  38.4 18.5 %all-to-all-start.3 = ((bf16[16,128,128]{2,1,0:T(8,128)(2,1)}), bf16[16,128,128]{2,1,0:T(8,128)(2,1)S(1)}, u32[]{:S(2)}, u32[]{:S(2)}) async-start(bf16[16,128,128]{2,1,0:T(8,128)(2,1)} %bitcast_bitcast_fusion), calls=%async_computation.3 | async-start | bytes 1048576 | tf_op jit(solution)/shard_map/all_to_all | solution.py:153
  46.8 1.3 %copy-start.5 = (f32[8,512,128]{2,1,0:T(8,128)}, f32[8,512,128]{2,1,0:T(8,128)S(1)}, u32[]{:S(2)}) copy-start(f32[8,512,128]{2,1,0:T(8,128)S(1)} %get-tuple-element.5.window_ref) | copy-start | bytes 6291460
  56.9 1.6 %copy-start.6 = (f32[8,512,128]{2,1,0:T(8,128)S(1)}, f32[8,512,128]{2,1,0:T(8,128)}, u32[]{:S(2)}) copy-start(f32[8,512,128]{2,1,0:T(8,128)} %copy-done.5) | copy-start | bytes 6291460
  75.0 17.9 %all-to-all-start.2 = ((bf16[16,128,128]{2,1,0:T(8,128)(2,1)}), bf16[16,128,128]{2,1,0:T(8,128)(2,1)S(1)}, u32[]{:S(2)}, u32[]{:S(2)}) async-start(bf16[16,128,128]{2,1,0:T(8,128)(2,1)} %bitcast.8), calls=%async_computation.2 | async-start | bytes 1048576 | tf_op jit(solution)/shard_map/all_to_all | solution.py:183

commit v2 on v1

v2 whole, which is shorter than its diff:
```python
import functools

import jax
import jax.numpy as jnp
import numpy as np
from jax import lax
from jax.experimental import pallas as pl
from jax.experimental.pallas import tpu as pltpu
from jax.sharding import PartitionSpec as P

F32 = jnp.float32
BF16 = jnp.bfloat16


def two_bf16(table):
    upper = table.astype(np.float32).astype(jnp.bfloat16)
    lower = (table - upper.astype(np.float64)).astype(np.float32).astype(jnp.bfloat16)
    return np.stack([upper, lower])


def dft_tables(block):
    freq = np.concatenate([np.arange(0, block, 2), np.arange(1, block, 2)])
    turns = ((2 * freq[:, None] + 1) * np.arange(block)[None, :]) % (4 * block)
    angle = turns * (np.pi / (2 * block))
    forward = np.concatenate([np.cos(angle), -np.sin(angle)], 0)
    return two_bf16(forward), two_bf16(forward.T / block)


def forward_dft(tables, block, columns):
    upper, lower = tables
    first = jnp.dot(upper[...], columns, preferred_element_type=F32)
    return first + jnp.dot(lower[...], columns, preferred_element_type=F32)


def inverse_dft(tables, spec):
    upper, lower = tables
    head = spec.astype(BF16)
    tail = (spec - head.astype(F32)).astype(BF16)
    total = jnp.dot(upper[...], head, preferred_element_type=F32)
    total += jnp.dot(lower[...], head, preferred_element_type=F32)
    return total + jnp.dot(upper[...], tail, preferred_element_type=F32)


def side_by_side(width):
    return 2 if width % 128 == 0 else 1


def spectra(tables, block, load, spec_ref):
    count, _, width = spec_ref.shape
    group = side_by_side(width)
    for j in range(0, count, group):
        parts = [load(j + u) for u in range(group)]
        both = forward_dft(tables, block, jnp.concatenate(parts, 1) if group > 1 else parts[0])
        for u in range(group):
            spec_ref[j + u] = both[:, u * width : (u + 1) * width]


def windows(block, spec_ref, window_ref):
    count = spec_ref.shape[0]
    half = block // 2
    for j in range(count):
        if j + 1 == count:
            window_ref[j] = spec_ref[j]
            continue
        for start, sign in ((0, 1), (half, -1)):
            real, imag = pl.ds(start, half), pl.ds(block + start, half)
            next_imag, next_real = spec_ref[j + 1, imag], spec_ref[j + 1, real]
            if sign > 0:
                window_ref[j, real] = spec_ref[j, real] + next_imag
                window_ref[j, imag] = spec_ref[j, imag] - next_real
            else:
                window_ref[j, real] = spec_ref[j, real] - next_imag
                window_ref[j, imag] = spec_ref[j, imag] + next_real


def correlate(block, left_ref, window_ref, out_ref):
    lefts, outs, count = left_ref.shape[0], out_ref.shape[0], window_ref.shape[0]

    def body(t, carry):
        real = pl.ds(pl.multiple_of(t * 8, 8), 8)
        imag = pl.ds(pl.multiple_of(block + t * 8, 8), 8)
        for a in range(outs):
            sum_real = sum_imag = None
            for s in range(min(lefts, count - a)):
                lr, li = left_ref[s, real], left_ref[s, imag]
                wr, wi = window_ref[a + s, real], window_ref[a + s, imag]
                re = lr * wr + li * wi
                im = lr * wi - li * wr
                sum_real = re if sum_real is None else sum_real + re
                sum_imag = im if sum_imag is None else sum_imag + im
            out_ref[a, real] = sum_real
            out_ref[a, imag] = sum_imag
        return carry

    lax.fori_loop(0, block // 8, body, 0)


def invert(tables, block, spec_ref, store):
    count, _, width = spec_ref.shape
    group = side_by_side(width)
    for j in range(0, count, group):
        parts = [spec_ref[j + u] for u in range(group)]
        both = inverse_dft(tables, jnp.concatenate(parts, 1) if group > 1 else parts[0])
        for u in range(group):
            store(j + u, both[:, u * width : (u + 1) * width].astype(BF16))


def fetch(pairs, sems):
    copies = [pltpu.make_async_copy(far, near, sems.at[k]) for k, (far, near) in enumerate(pairs)]
    for copy in copies:
        copy.start()
    return copies


def half_of(ref, rows, half):
    def load(j):
        return jnp.concatenate([ref[2 * j + u, pl.ds(half * rows, rows), :] for u in range(2)], 0)

    return load


def both_grads(block, loads, stores, refs):
    forward, inverse, fv, iv, spec, window, tap_spec, tap_sum, sems = refs
    copies = fetch([(forward, fv), (inverse, iv)], sems)
    load_grad, load_value, load_taps = loads()
    ahead, back = (fv.at[0], fv.at[1]), (iv.at[0], iv.at[1])
    copies[0].wait()
    spectra(ahead, block, load_grad, spec)
    windows(block, spec, window)
    spectra(ahead, block, load_value, spec)
    correlate(block, spec, window, tap_sum)
    spectra(ahead, block, load_taps, tap_spec)
    correlate(block, tap_spec, window, spec)
    copies[1].wait()
    invert(back, block, tap_sum, stores[1])
    invert(back, block, spec, stores[0])


def plain_kernel(block, sent_ref, taps_ref, forward, inverse, grad_ref, tap_grad_ref, *refs):
    rows = block // 2

    def loads():
        return (
            half_of(sent_ref, rows, 0),
            half_of(sent_ref, rows, 1),
            lambda j: taps_ref[pl.ds(j * block, block), :],
        )

    def store_grad(j, result):
        for u in range(2):
            grad_ref[2 * j + u] = result[u * rows : (u + 1) * rows]

    def store_taps(j, result):
        tap_grad_ref[pl.ds(j * block, block), :] = result

    both_grads(block, loads, (store_grad, store_taps), (forward, inverse, *refs))


def traded(top, bottom):
    half = top.shape[1] // 2
    left = lax.broadcasted_iota(jnp.int32, top.shape, 1) < half
    return (
        jnp.where(left, top, pltpu.roll(bottom, half, 1)),
        jnp.where(left, pltpu.roll(top, half, 1), bottom),
    )


def pack_kernel(grad_ref, value_ref, taps_ref, out_ref):
    half = grad_ref.shape[0] // 2
    own, size = out_ref.shape[2], taps_ref.shape[2]
    for i in range(out_ref.shape[0] // 2):
        columns = pl.ds(i * own, own)
        for n, ref in enumerate((grad_ref, value_ref)):
            pair = traded(ref[pl.ds(0, half), columns].astype(F32), ref[pl.ds(half, half), columns].astype(F32))
            for j in range(2):
                out_ref[2 * i + j, pl.ds(n * half, half), :] = pair[j].astype(BF16)
        pair = traded(taps_ref[0, i].astype(F32), taps_ref[1, i].astype(F32))
        for j in range(2):
            out_ref[2 * i + j, pl.ds(2 * half, size), :] = pair[j].astype(BF16)


def paired_kernel(sizes, sent_ref, forward, inverse, out_ref, whole, taps, *refs):
    block, tap_rows, tap_segs = sizes
    rows, half = block // 2, block // 4
    count = sent_ref.shape[0] // 2
    size = tap_rows * tap_segs

    def loads():
        for i in range(count):
            for n in range(2):
                pair = [sent_ref[2 * i + j, pl.ds(n * half, half), :].astype(F32) for j in range(2)]
                for u, part in enumerate(traded(*pair)):
                    whole[n, pl.ds(i * rows + u * half, half), :] = part.astype(BF16)
            for j in range(2):
                piece = sent_ref[2 * i + j, pl.ds(2 * half, size), :].astype(F32)
                for s in range(tap_segs):
                    taps[j * tap_segs + s, pl.ds(i * tap_rows, tap_rows), :] = piece[s * tap_rows : (s + 1) * tap_rows]
        return (
            lambda j: whole[0, pl.ds(j * block, block), :],
            lambda j: whole[1, pl.ds(j * block, block), :],
            lambda j: jnp.concatenate([taps[2 * j + u].astype(BF16) for u in range(2)], 0),
        )

    def store_grad(j, result):
        for u in range(2):
            at = u * rows
            result32 = result.astype(F32)
            pair = traded(result32[at : at + half], result32[at + half : at + rows])
            for side in range(2):
                out_ref[2 * (2 * j + u) + side, pl.ds(0, half), :] = pair[side].astype(BF16)

    def store_taps(j, result):
        for u in range(2):
            taps[2 * j + u] = result[u * rows : (u + 1) * rows].astype(F32)
        if 2 * j + 2 < taps.shape[0]:
            return
        for i in range(count):
            for side in range(2):
                pieces = [taps[side * tap_segs + s, pl.ds(i * tap_rows, tap_rows), :] for s in range(tap_segs)]
                out_ref[2 * i + side, pl.ds(half, size), :] = jnp.concatenate(pieces, 0).astype(BF16)

    both_grads(block, loads, (store_grad, store_taps), (forward, inverse, *refs))


def unpack_kernel(sizes, back_ref, grad_ref, taps_ref):
    tap_rows, tap_segs = sizes
    rows, width = grad_ref.shape
    half, own = rows // 2, back_ref.shape[2]
    size = tap_rows * tap_segs
    for i in range(back_ref.shape[0] // 2):
        pair = traded(*[back_ref[2 * i + j, pl.ds(0, half), :].astype(F32) for j in range(2)])
        for u in range(2):
            grad_ref[pl.ds(u * half, half), pl.ds(i * own, own)] = pair[u].astype(BF16)
        pair = traded(*[back_ref[2 * i + j, pl.ds(half, size), :].astype(F32) for j in range(2)])
        for side in range(2):
            for s in range(tap_segs):
                taps_ref[:, s, pl.ds(side * width + i * own, own)] = pair[side][s * tap_rows : (s + 1) * tap_rows]


def split_kernel(*refs):
    ins, out_ref = refs[:-1], refs[-1]
    count, size, own = out_ref.shape
    rows = size // len(ins)
    for k in range(count):
        for n, ref in enumerate(ins):
            out_ref[k, pl.ds(n * rows, rows), :] = ref[:, k * own : (k + 1) * own]


def call_kernel(body, out_shape, operands, scratch=(), flops=0, far=(), sems=0):
    held = [a for k, a in enumerate(operands) if k not in far]
    held += list(out_shape) + list(scratch)
    padded = sum(int(np.prod(a.shape[:-1])) * max(a.shape[-1], 128) * a.dtype.itemsize for a in held)
    moved = sum(int(np.prod(a.shape)) * a.dtype.itemsize for a in list(operands) + list(out_shape))
    near, away = pl.BlockSpec(memory_space=pltpu.VMEM), pl.BlockSpec(memory_space=pl.ANY)
    scratch_shapes = [pltpu.VMEM(a.shape, a.dtype) for a in scratch]
    if sems:
        scratch_shapes.append(pltpu.SemaphoreType.DMA((sems,)))
    return pl.pallas_call(
        body,
        out_shape=out_shape,
        in_specs=[away if k in far else near for k in range(len(operands))],
        out_specs=[near] * len(out_shape),
        scratch_shapes=scratch_shapes,
        compiler_params=pltpu.CompilerParams(vmem_limit_bytes=min(padded + (6 << 20), 56 << 20)),
        cost_estimate=pl.CostEstimate(flops=flops, bytes_accessed=moved, transcendentals=0),
    )(*operands)


def shards(grad_out, inputs, filter_taps):
    rows, width = grad_out.shape
    ctx, ch = lax.axis_size("ctx"), lax.axis_size("ch")
    tap_rows, tap_segs, channels = filter_taps.shape
    own = width // ctx
    block = 2 * rows
    taps = rows * tap_segs * ch
    size = tap_rows * tap_segs
    blocks, tap_blocks = rows * ctx // block, taps // block
    shape = jax.ShapeDtypeStruct
    paired = own == 128 and ch == 2 and rows % 32 == 0 and tap_rows % 8 == 0 and size % 16 == 0

    forward, inverse = (jnp.asarray(t) for t in dft_tables(block))
    spec = shape((blocks, 2 * block, own), F32)
    tap_spec = shape((tap_blocks, 2 * block, own), F32)
    scratch = [shape(forward.shape, BF16), shape(inverse.shape, BF16), spec, spec, tap_spec, tap_spec]
    flops = 4 * block * block * own * 5 * (blocks + tap_blocks)
    tap_parts = filter_taps.reshape(tap_rows, tap_segs, ch, ctx, own)

    if paired:
        tap_parts = tap_parts.transpose(2, 3, 1, 0, 4).reshape(ch, ctx, size, own)
        (sent,) = call_kernel(
            pack_kernel, [shape((ctx * ch, rows + size, own), BF16)], (grad_out, inputs, tap_parts)
        )
        sent = lax.all_to_all(sent, ("ctx", "ch"), 0, 0, tiled=True)
        (back,) = call_kernel(
            functools.partial(paired_kernel, (block, tap_rows, tap_segs)),
            [shape((ctx * ch, rows // 2 + size, own), BF16)],
            (sent, forward, inverse),
            [shape((2, rows * ctx, own), BF16), shape((ch * tap_segs, rows, own), F32)] + scratch,
            flops,
            (1, 2),
            sems=2,
        )
        back = lax.all_to_all(back, ("ctx", "ch"), 0, 0, tiled=True)
        return call_kernel(
            functools.partial(unpack_kernel, (tap_rows, tap_segs)),
            [shape((rows, width), BF16), shape(filter_taps.shape, F32)],
            (back,),
        )

    (sent,) = call_kernel(split_kernel, [shape((ctx, 2 * rows, own), BF16)], (grad_out, inputs))
    sent = lax.all_to_all(sent, "ctx", 0, 0, tiled=True)
    tap_parts = tap_parts.transpose(3, 2, 0, 1, 4).reshape(ctx * ch, tap_rows, tap_segs, own)
    tap_parts = lax.all_to_all(tap_parts, ("ctx", "ch"), 0, 0, tiled=True)
    tap_all = tap_parts.reshape(ctx, ch, tap_rows, tap_segs, own).transpose(1, 3, 0, 2, 4)
    input_grad, tap_grad = call_kernel(
        functools.partial(plain_kernel, block),
        [shape((ctx, rows, own), BF16), shape((taps, own), BF16)],
        (sent, tap_all.reshape(taps, own), forward, inverse),
        scratch,
        flops,
        (2, 3),
        sems=2,
    )
    back = lax.all_to_all(input_grad, "ctx", 0, 0, tiled=True)
    grad_inputs = back.transpose(1, 0, 2).reshape(rows, width)
    out_parts = tap_grad.reshape(ch, tap_segs, ctx, tap_rows, own).transpose(2, 0, 3, 1, 4)
    out_parts = out_parts.reshape(ctx * ch, tap_rows, tap_segs, own)
    out_parts = lax.all_to_all(out_parts, ("ctx", "ch"), 0, 0, tiled=True)
    out_parts = out_parts.reshape(ctx, ch, tap_rows, tap_segs, own).transpose(2, 3, 1, 0, 4)
    grad_taps = out_parts.reshape(tap_rows, tap_segs, channels).astype(F32)
    return grad_inputs, grad_taps


def solution(mesh):
    return jax.shard_map(
        shards,
        mesh=mesh,
        in_specs=(P("ctx", "ch"), P("ctx", "ch"), P("ctx", "ch", None)),
        out_specs=(P("ctx", "ch"), P("ctx", "ch", None)),
        check_vma=False,
    )
```

time: 94.8 us -> 73.7 us (0.78)
  blocking collectives: 13.9 us -> 63.1 us
  waiting for transfers between devices: 44.4 us -> 0 us
  starting transfers between devices: 19 us -> 0 us
  local copies, waits for them, and re-layouts: 9.28 us -> 1.52 us
  Pallas kernels: 6.41 us -> 8.2 us
    all_to_all x1 -> x2, blocking collectives: 13.9 us -> 63.1 us  [the longest x1 39.9 us: shards(): sent = lax.all_to_all(sent, ('ctx', 'ch'), 0, 0, tiled=True)]
    all_to_all x4 -> x0, waiting for transfers between devices: 44.4 us -> none  [the longest x2 22 us: to_channels(): return lax.all_to_all(parts, 'ctx', 0, 0, tiled=True).reshape(length, own)]
    all_to_all x4 -> x0, starting transfers between devices: 19 us -> none  [the longest x2 8.19 us: to_channels(): return lax.all_to_all(parts, 'ctx', 0, 0, tiled=True).reshape(length, own)]
    unnamed x18 -> x8, local copies, waits for them, and re-layouts: 4.23 us -> 0.02 us
    transpose x4 -> x0, local copies, waits for them, and re-layouts: 2.81 us -> none  [the longest x2 1.88 us: to_channels(): parts = array.reshape(rows, ctx, own).transpose(1, 0, 2)]
    pallas_call x2 -> x3, Pallas kernels: 6.41 us -> 8.2 us  [call_kernel(): pl.pallas_call(body, out_shape=out_shape, in_specs=[away if k in far else...]
    reshape x3 -> x2, local copies, waits for them, and re-layouts: 2.25 us -> 1.49 us  [shards(): tap_parts = filter_taps.reshape(tap_rows, tap_segs, ch, ctx, own)]
  transfers between devices with their start and end apart: 4 -> 0, of which waited for: 4 -> 0; matrix products, arithmetic and copies ran while one was open for 3% -> 0% of each run, Pallas kernels for 4% -> 0%
where the time goes in v2:
time: 73.7 us; the launch traced here: 73.5 us
  blocking collectives  63.1 us (86%)
  Pallas kernels  8.2 us (11%)
  local copies, waits for them, and re-layouts  1.52 us (2%)
    all_to_all x1, blocking collectives, shards(): sent = lax.all_to_all(sent, ('ctx', 'ch'), 0, 0, tiled=True)  39.9 us
    all_to_all x1, blocking collectives, shards(): back = lax.all_to_all(back, ('ctx', 'ch'), 0, 0, tiled=True)  23.2 us
    pallas_call x3, Pallas kernels, call_kernel(): pl.pallas_call(body, out_shape=out_shape, in_specs=[away if k in far else...  8.2 us
    reshape x2, local copies, waits for them, and re-layouts, shards(): tap_parts = filter_taps.reshape(tap_rows, tap_segs, ch, ctx, own)  1.49 us

profile of v2, /device:TPU:1, one launch (start us, length us, event | category | flops | bytes accessed | tf_op | source)
XLA Modules:
  0.0 73.5 jit_solution(14006312577427872862)
XLA Ops:
  0.6 0.0 copy-start.1
  0.6 0.0 copy-start
  0.6 1.3 %reshape.10 = bf16[8,4,2,16,128]{4,3,2,1,0:T(8,128)(2,1)S(1)} reshape(bf16[8,4,4096]{2,1,0:T(4,128)(2,1)} %param.7) | data formatting | bytes 524288 | tf_op jit(solution)/shard_map/reshape | solution.py:286
  2.0 0.2 copy.9
  2.2 0.0 copy-done.1
  2.2 0.0 copy-done
  2.2 0.5 shard_map.68
  2.7 0.0 copy-start.2
  2.7 0.0 copy-start.3
  2.7 39.9 %all_to_all.10.sent_ref = bf16[32,160,128]{2,1,0:T(8,128)(2,1)S(1)} all-to-all(bf16[32,160,128]{2,1,0:T(8,128)(2,1)S(1)} %shard_map.68), channel_id=1, replica_groups=mesh['ctx'=16,'ch'=2] {'ctx','ch'}, dimensions={0} | all-to-all | bytes 2621440 | tf_op jit(solution)/shard_map/all_to_all | solution.py:293
  42.6 0.0 copy-done.2
  42.6 0.0 copy-done.3
  42.6 6.1 %shard_map.69 = bf16[32,96,128]{2,1,0:T(8,128)(2,1)S(1)} custom-call(bf16[32,160,128]{2,1,0:T(8,128)(2,1)S(1)} %all_to_all.10.sent_ref, bf16[2,512,256]{2,1,0:T(8,128)(2,1)S(1)} %copy-done.3, bf16[2,256,512]{2,1,0:T(8,128)(2,1)S(1)} %copy-done.2), custom_call_target="tpu_custom_call" | custom-call | flops 2013265920 | bytes 3145728 | tf_op jit(solution)/shard_map/pallas_call | solution.py:258
  48.8 23.2 %all_to_all.11.back_ref = bf16[32,96,128]{2,1,0:T(8,128)(2,1)S(1)} all-to-all(bf16[32,96,128]{2,1,0:T(8,128)(2,1)S(1)} %shard_map.69), channel_id=1, replica_groups=mesh['ctx'=16,'ch'=2] {'ctx','ch'}, dimensions={0} | all-to-all | bytes 1572864 | tf_op jit(solution)/shard_map/all_to_all | solution.py:303
  72.0 1.5 %shard_map.70 = (bf16[128,2048]{1,0:T(8,128)(2,1)}, f32[8,4,4096]{2,1,0:T(4,128)}) custom-call(bf16[32,96,128]{2,1,0:T(8,128)(2,1)S(1)} %all_to_all.11.back_ref), custom_call_target="tpu_custom_call" | custom-call | bytes 1835008 | tf_op jit(solution)/shard_map/pallas_call | solution.py:258
Async XLA Ops:
  0.6 1.5 %copy-start.1 = (bf16[128,2048]{1,0:T(8,128)(2,1)S(1)}, bf16[128,2048]{1,0:T(8,128)(2,1)}, u32[]{:S(2)}) copy-start(bf16[128,2048]{1,0:T(8,128)(2,1)} %value_ref.1) | copy-start | bytes 1572868
  0.6 1.5 %copy-start = (bf16[128,2048]{1,0:T(8,128)(2,1)S(1)}, bf16[128,2048]{1,0:T(8,128)(2,1)}, u32[]{:S(2)}) copy-start(bf16[128,2048]{1,0:T(8,128)(2,1)} %grad_ref.1) | copy-start | bytes 1572868
  2.7 39.9 %copy-start.2 = (bf16[2,256,512]{2,1,0:T(8,128)(2,1)S(1)}, bf16[2,256,512]{2,1,0:T(8,128)(2,1)}, u32[]{:S(2)}) copy-start(bf16[2,256,512]{2,1,0:T(8,128)(2,1)} %constant.5.clone.inverse) | copy-start | bytes 1572868
  2.7 39.9 %copy-start.3 = (bf16[2,512,256]{2,1,0:T(8,128)(2,1)S(1)}, bf16[2,512,256]{2,1,0:T(8,128)(2,1)}, u32[]{:S(2)}) copy-start(bf16[2,512,256]{2,1,0:T(8,128)(2,1)} %constant.4.clone.forward) | copy-start | bytes 1572868

commit v3 on v2

--- a/solution.py
+++ b/solution.py
@@ -26,83 +26,92 @@
     return two_bf16(forward), two_bf16(forward.T / block)
 
 
-def forward_dft(tables, block, columns):
-    upper, lower = tables
-    first = jnp.dot(upper[...], columns, preferred_element_type=F32)
-    return first + jnp.dot(lower[...], columns, preferred_element_type=F32)
-
-
-def inverse_dft(tables, spec):
-    upper, lower = tables
+def forward_dft(table, columns):
+    first = jnp.dot(table[0], columns, preferred_element_type=F32)
+    return first + jnp.dot(table[1], columns, preferred_element_type=F32)
+
+
+def inverse_dft(table, spec):
     head = spec.astype(BF16)
     tail = (spec - head.astype(F32)).astype(BF16)
-    total = jnp.dot(upper[...], head, preferred_element_type=F32)
-    total += jnp.dot(lower[...], head, preferred_element_type=F32)
-    return total + jnp.dot(upper[...], tail, preferred_element_type=F32)
+    total = jnp.dot(table[0], head, preferred_element_type=F32)
+    total += jnp.dot(table[1], head, preferred_element_type=F32)
+    return total + jnp.dot(table[0], tail, preferred_element_type=F32)
 
 
 def side_by_side(width):
     return 2 if width % 128 == 0 else 1
 
 
-def spectra(tables, block, load, spec_ref):
+def spectra(table, block, load, spec_ref):
     count, _, width = spec_ref.shape
     group = side_by_side(width)
-    for j in range(0, count, group):
+
+    def step(j):
         parts = [load(j + u) for u in range(group)]
-        both = forward_dft(tables, block, jnp.concatenate(parts, 1) if group > 1 else parts[0])
+        both = forward_dft(table, jnp.concatenate(parts, 1) if group > 1 else parts[0])
         for u in range(group):
             spec_ref[j + u] = both[:, u * width : (u + 1) * width]
 
-
-def windows(block, spec_ref, window_ref):
-    count = spec_ref.shape[0]
-    half = block // 2
-    for j in range(count):
-        if j + 1 == count:
-            window_ref[j] = spec_ref[j]
-            continue
-        for start, sign in ((0, 1), (half, -1)):
-            real, imag = pl.ds(start, half), pl.ds(block + start, half)
-            next_imag, next_real = spec_ref[j + 1, imag], spec_ref[j + 1, real]
-            if sign > 0:
-                window_ref[j, real] = spec_ref[j, real] + next_imag
-                window_ref[j, imag] = spec_ref[j, imag] - next_real
-            else:
-                window_ref[j, real] = spec_ref[j, real] - next_imag
-                window_ref[j, imag] = spec_ref[j, imag] + next_real
-
-
-def correlate(block, left_ref, window_ref, out_ref):
-    lefts, outs, count = left_ref.shape[0], out_ref.shape[0], window_ref.shape[0]
-
-    def body(t, carry):
-        real = pl.ds(pl.multiple_of(t * 8, 8), 8)
-        imag = pl.ds(pl.multiple_of(block + t * 8, 8), 8)
+    return [functools.partial(step, j) for j in range(0, count, group)]
+
+
+def correlate(block, left_ref, grad_ref, out_ref, beside=()):
+    lefts, outs, count = left_ref.shape[0], out_ref.shape[0], grad_ref.shape[0]
+    tiles = block // 8
+
+    def pieces(ref, real, imag):
+        return [(ref[j, real], ref[j, imag]) for j in range(ref.shape[0])]
+
+    def tile(sign, real, imag):
+        grad, left = pieces(grad_ref, real, imag), pieces(left_ref, real, imag)
+        window = []
+        for j in range(count):
+            re, im = grad[j]
+            if j + 1 < count:
+                next_re, next_im = grad[j + 1]
+                re, im = (re + next_im, im - next_re) if sign > 0 else (re - next_im, im + next_re)
+            window.append((re, im))
         for a in range(outs):
             sum_real = sum_imag = None
-            for s in range(min(lefts, count - a)):
-                lr, li = left_ref[s, real], left_ref[s, imag]
-                wr, wi = window_ref[a + s, real], window_ref[a + s, imag]
-                re = lr * wr + li * wi
-                im = lr * wi - li * wr
+            for (lr, li), (wr, wi) in zip(left, window[a:]):
+                re, im = lr * wr + li * wi, lr * wi - li * wr
                 sum_real = re if sum_real is None else sum_real + re
                 sum_imag = im if sum_imag is None else sum_imag + im
-            out_ref[a, real] = sum_real
-            out_ref[a, imag] = sum_imag
+            out_ref[a, real], out_ref[a, imag] = sum_real, sum_imag
+
+    def body(sign, first, t, carry):
+        at = pl.multiple_of(first + t * 8, 8)
+        tile(sign, pl.ds(at, 8), pl.ds(pl.multiple_of(block + at, 8), 8))
         return carry
 
-    lax.fori_loop(0, block // 8, body, 0)
-
-
-def invert(tables, block, spec_ref, store):
+    if not beside:
+        for sign, first in ((1, 0), (-1, block // 2)):
+            lax.fori_loop(0, tiles // 2, functools.partial(body, sign, first), 0)
+        return
+    each = tiles // len(beside)
+    for k, step in enumerate(beside):
+        step()
+        for t in range(k * each, (k + 1) * each):
+            tile(1 if 2 * t < tiles else -1, pl.ds(t * 8, 8), pl.ds(block + t * 8, 8))
+
+
+def invert(table, block, spec_ref, store):
     count, _, width = spec_ref.shape
     group = side_by_side(width)
-    for j in range(0, count, group):
+
+    def step(j):
         parts = [spec_ref[j + u] for u in range(group)]
-        both = inverse_dft(tables, jnp.concatenate(parts, 1) if group > 1 else parts[0])
+        both = inverse_dft(table, jnp.concatenate(parts, 1) if group > 1 else parts[0])
         for u in range(group):
             store(j + u, both[:, u * width : (u + 1) * width].astype(BF16))
+
+    return [functools.partial(step, j) for j in range(0, count, group)]
+
+
+def run(steps):
+    for step in steps:
+        step()
 
 
 def fetch(pairs, sems):
@@ -120,31 +129,37 @@
 
 
 def both_grads(block, loads, stores, refs):
-    forward, inverse, fv, iv, spec, window, tap_spec, tap_sum, sems = refs
+    forward, inverse, fv, iv, grad_spec, value_spec, spec, tap_spec, tap_sum, sems = refs
     copies = fetch([(forward, fv), (inverse, iv)], sems)
-    load_grad, load_value, load_taps = loads()
-    ahead, back = (fv.at[0], fv.at[1]), (iv.at[0], iv.at[1])
+    (ready_grad, load_grad), (ready_value, load_value), (ready_taps, load_taps) = loads
+    ready_grad()
     copies[0].wait()
-    spectra(ahead, block, load_grad, spec)
-    windows(block, spec, window)
-    spectra(ahead, block, load_value, spec)
-    correlate(block, spec, window, tap_sum)
-    spectra(ahead, block, load_taps, tap_spec)
-    correlate(block, tap_spec, window, spec)
     copies[1].wait()
-    invert(back, block, tap_sum, stores[1])
-    invert(back, block, spec, stores[0])
+    ready_taps()
+    run(spectra(fv, block, load_grad, grad_spec))
+    ready_value()
+    run(spectra(fv, block, load_taps, tap_spec))
+    value_steps = spectra(fv, block, load_value, value_spec)
+    grad_steps = invert(iv, block, spec, stores[0])
+    if len(value_steps) > 8:
+        run(value_steps)
+        value_steps = ()
+    correlate(block, tap_spec, grad_spec, spec, value_steps)
+    if len(grad_steps) > 8:
+        run(grad_steps)
+        grad_steps = ()
+    correlate(block, value_spec, grad_spec, tap_sum, grad_steps)
+    run(invert(iv, block, tap_sum, stores[1]))
 
 
 def plain_kernel(block, sent_ref, taps_ref, forward, inverse, grad_ref, tap_grad_ref, *refs):
     rows = block // 2
 
-    def loads():
-        return (
-            half_of(sent_ref, rows, 0),
-            half_of(sent_ref, rows, 1),
-            lambda j: taps_ref[pl.ds(j * block, block), :],
-        )
+    loads = (
+        (tuple, half_of(sent_ref, rows, 0)),
+        (tuple, half_of(sent_ref, rows, 1)),
+        (tuple, lambda j: taps_ref[pl.ds(j * block, block), :]),
+    )
 
     def store_grad(j, result):
         for u in range(2):
@@ -180,26 +195,29 @@
 
 
 def paired_kernel(sizes, sent_ref, forward, inverse, out_ref, whole, taps, *refs):
-    block, tap_rows, tap_segs = sizes
+    block, size, tap_segs = sizes
     rows, half = block // 2, block // 4
     count = sent_ref.shape[0] // 2
-    size = tap_rows * tap_segs
-
-    def loads():
+
+    def untrade(n):
         for i in range(count):
-            for n in range(2):
-                pair = [sent_ref[2 * i + j, pl.ds(n * half, half), :].astype(F32) for j in range(2)]
-                for u, part in enumerate(traded(*pair)):
-                    whole[n, pl.ds(i * rows + u * half, half), :] = part.astype(BF16)
+            pair = [sent_ref[2 * i + j, pl.ds(n * half, half), :].astype(F32) for j in range(2)]
+            for u, part in enumerate(traded(*pair)):
+                whole[n, pl.ds(i * rows + u * half, half), :] = part.astype(BF16)
+
+    def gather_taps():
+        for i in range(count):
             for j in range(2):
-                piece = sent_ref[2 * i + j, pl.ds(2 * half, size), :].astype(F32)
-                for s in range(tap_segs):
-                    taps[j * tap_segs + s, pl.ds(i * tap_rows, tap_rows), :] = piece[s * tap_rows : (s + 1) * tap_rows]
-        return (
-            lambda j: whole[0, pl.ds(j * block, block), :],
-            lambda j: whole[1, pl.ds(j * block, block), :],
-            lambda j: jnp.concatenate([taps[2 * j + u].astype(BF16) for u in range(2)], 0),
-        )
+                taps[j, pl.ds(i * size, size), :] = sent_ref[2 * i + j, pl.ds(2 * half, size), :].astype(F32)
+
+    loads = (
+        (functools.partial(untrade, 0), lambda j: whole[0, pl.ds(j * block, block), :]),
+        (functools.partial(untrade, 1), lambda j: whole[1, pl.ds(j * block, block), :]),
+        (gather_taps, lambda j: jnp.concatenate([taps[segment(2 * j + u)].astype(BF16) for u in range(2)], 0)),
+    )
+
+    def segment(s):
+        return s // tap_segs, pl.ds(s % tap_segs, rows, stride=tap_segs), slice(None)
 
     def store_grad(j, result):
         for u in range(2):
@@ -211,21 +229,20 @@
 
     def store_taps(j, result):
         for u in range(2):
-            taps[2 * j + u] = result[u * rows : (u + 1) * rows].astype(F32)
-        if 2 * j + 2 < taps.shape[0]:
+            taps[segment(2 * j + u)] = result[u * rows : (u + 1) * rows].astype(F32)
+        if (2 * j + 2) % tap_segs:
             return
+        side = 2 * j // tap_segs
         for i in range(count):
-            for side in range(2):
-                pieces = [taps[side * tap_segs + s, pl.ds(i * tap_rows, tap_rows), :] for s in range(tap_segs)]
-                out_ref[2 * i + side, pl.ds(half, size), :] = jnp.concatenate(pieces, 0).astype(BF16)
+            out_ref[2 * i + side, pl.ds(half, size), :] = taps[side, pl.ds(i * size, size), :].astype(BF16)
 
     both_grads(block, loads, (store_grad, store_taps), (forward, inverse, *refs))
 
 
-def unpack_kernel(sizes, back_ref, grad_ref, taps_ref):
-    tap_rows, tap_segs = sizes
+def unpack_kernel(back_ref, grad_ref, taps_ref):
     rows, width = grad_ref.shape
     half, own = rows // 2, back_ref.shape[2]
+    tap_rows, tap_segs = taps_ref.shape[:2]
     size = tap_rows * tap_segs
     for i in range(back_ref.shape[0] // 2):
         pair = traded(*[back_ref[2 * i + j, pl.ds(0, half), :].astype(F32) for j in range(2)])
@@ -233,8 +250,7 @@
             grad_ref[pl.ds(u * half, half), pl.ds(i * own, own)] = pair[u].astype(BF16)
         pair = traded(*[back_ref[2 * i + j, pl.ds(half, size), :].astype(F32) for j in range(2)])
         for side in range(2):
-            for s in range(tap_segs):
-                taps_ref[:, s, pl.ds(side * width + i * own, own)] = pair[side][s * tap_rows : (s + 1) * tap_rows]
+            taps_ref[:, :, pl.ds(side * width + i * own, own)] = pair[side].reshape(tap_rows, tap_segs, own)
 
 
 def split_kernel(*refs):
@@ -276,33 +292,33 @@
     size = tap_rows * tap_segs
     blocks, tap_blocks = rows * ctx // block, taps // block
     shape = jax.ShapeDtypeStruct
-    paired = own == 128 and ch == 2 and rows % 32 == 0 and tap_rows % 8 == 0 and size % 16 == 0
+    paired = own == 128 and ch == 2 and rows % 32 == 0 and size % 16 == 0 and tap_segs % 2 == 0
 
     forward, inverse = (jnp.asarray(t) for t in dft_tables(block))
     spec = shape((blocks, 2 * block, own), F32)
     tap_spec = shape((tap_blocks, 2 * block, own), F32)
-    scratch = [shape(forward.shape, BF16), shape(inverse.shape, BF16), spec, spec, tap_spec, tap_spec]
+    scratch = [shape(forward.shape, BF16), shape(inverse.shape, BF16), spec, spec, spec, tap_spec, tap_spec]
     flops = 4 * block * block * own * 5 * (blocks + tap_blocks)
     tap_parts = filter_taps.reshape(tap_rows, tap_segs, ch, ctx, own)
 
     if paired:
-        tap_parts = tap_parts.transpose(2, 3, 1, 0, 4).reshape(ch, ctx, size, own)
+        tap_parts = tap_parts.transpose(2, 3, 0, 1, 4).reshape(ch, ctx, size, own)
         (sent,) = call_kernel(
             pack_kernel, [shape((ctx * ch, rows + size, own), BF16)], (grad_out, inputs, tap_parts)
         )
         sent = lax.all_to_all(sent, ("ctx", "ch"), 0, 0, tiled=True)
         (back,) = call_kernel(
-            functools.partial(paired_kernel, (block, tap_rows, tap_segs)),
+            functools.partial(paired_kernel, (block, size, tap_segs)),
             [shape((ctx * ch, rows // 2 + size, own), BF16)],
             (sent, forward, inverse),
-            [shape((2, rows * ctx, own), BF16), shape((ch * tap_segs, rows, own), F32)] + scratch,
+            [shape((2, rows * ctx, own), BF16), shape((ch, rows * tap_segs, own), F32)] + scratch,
             flops,
             (1, 2),
             sems=2,
         )
         back = lax.all_to_all(back, ("ctx", "ch"), 0, 0, tiled=True)
         return call_kernel(
-            functools.partial(unpack_kernel, (tap_rows, tap_segs)),
+            unpack_kernel,
             [shape((rows, width), BF16), shape(filter_taps.shape, F32)],
             (back,),
         )

time: 73.7 us -> 71.5 us (0.970)
  Pallas kernels: 8.2 us -> 6.09 us
    pallas_call x3, Pallas kernels: 8.2 us -> 6.09 us  [call_kernel(): pl.pallas_call(body, out_shape=out_shape, in_specs=[away if k in far else...]
where the time goes in v3:
time: 71.5 us; the launch traced here: 71.4 us
  blocking collectives  63.1 us (88%)
  Pallas kernels  6.09 us (9%)
  local copies, waits for them, and re-layouts  1.48 us (2%)
    all_to_all x1, blocking collectives, shards(): sent = lax.all_to_all(sent, ('ctx', 'ch'), 0, 0, tiled=True)  39.9 us
    all_to_all x1, blocking collectives, shards(): back = lax.all_to_all(back, ('ctx', 'ch'), 0, 0, tiled=True)  23.2 us
    pallas_call x3, Pallas kernels, call_kernel(): pl.pallas_call(body, out_shape=out_shape, in_specs=[away if k in far else...  6.09 us
    reshape x2, local copies, waits for them, and re-layouts, shards(): tap_parts = filter_taps.reshape(tap_rows, tap_segs, ch, ctx, own)  1.45 us

profile of v3, /device:TPU:1, one launch (start us, length us, event | category | flops | bytes accessed | tf_op | source)
XLA Modules:
  0.0 71.4 jit_solution(16151601564459382465)
XLA Ops:
  0.6 0.0 copy-start.1
  0.6 0.0 copy-start
  0.6 1.3 %reshape.10 = bf16[8,4,2,16,128]{4,3,2,1,0:T(8,128)(2,1)S(1)} reshape(bf16[8,4,4096]{2,1,0:T(4,128)(2,1)} %param.7) | data formatting | bytes 524288 | tf_op jit(solution)/shard_map/reshape | solution.py:302
  2.0 0.1 copy.7
  2.1 0.0 copy-done.1
  2.1 0.0 copy-done
  2.1 0.5 shard_map.68
  2.7 0.0 copy-start.2
  2.7 0.0 copy-start.3
  2.7 39.9 %all_to_all.10.sent_ref = bf16[32,160,128]{2,1,0:T(8,128)(2,1)S(1)} all-to-all(bf16[32,160,128]{2,1,0:T(8,128)(2,1)S(1)} %shard_map.68), channel_id=1, replica_groups=mesh['ctx'=16,'ch'=2] {'ctx','ch'}, dimensions={0} | all-to-all | bytes 2621440 | tf_op jit(solution)/shard_map/all_to_all | solution.py:309
  42.6 0.0 copy-done.2
  42.6 0.0 copy-done.3
  42.6 4.2 %shard_map.69 = bf16[32,96,128]{2,1,0:T(8,128)(2,1)S(1)} custom-call(bf16[32,160,128]{2,1,0:T(8,128)(2,1)S(1)} %all_to_all.10.sent_ref, bf16[2,512,256]{2,1,0:T(8,128)(2,1)S(1)} %copy-done.3, bf16[2,256,512]{2,1,0:T(8,128)(2,1)S(1)} %copy-done.2), custom_call_target="tpu_custom_call" | custom-call | flops 2013265920 | bytes 3145728 | tf_op jit(solution)/shard_map/pallas_call | solution.py:274
  46.8 23.2 %all_to_all.11.back_ref = bf16[32,96,128]{2,1,0:T(8,128)(2,1)S(1)} all-to-all(bf16[32,96,128]{2,1,0:T(8,128)(2,1)S(1)} %shard_map.69), channel_id=1, replica_groups=mesh['ctx'=16,'ch'=2] {'ctx','ch'}, dimensions={0} | all-to-all | bytes 1572864 | tf_op jit(solution)/shard_map/all_to_all | solution.py:319
  70.0 1.4 %shard_map.70 = (bf16[128,2048]{1,0:T(8,128)(2,1)}, f32[8,4,4096]{2,1,0:T(4,128)}) custom-call(bf16[32,96,128]{2,1,0:T(8,128)(2,1)S(1)} %all_to_all.11.back_ref), custom_call_target="tpu_custom_call" | custom-call | bytes 1835008 | tf_op jit(solution)/shard_map/pallas_call | solution.py:274
Async XLA Ops:
  0.6 1.5 %copy-start.1 = (bf16[128,2048]{1,0:T(8,128)(2,1)S(1)}, bf16[128,2048]{1,0:T(8,128)(2,1)}, u32[]{:S(2)}) copy-start(bf16[128,2048]{1,0:T(8,128)(2,1)} %value_ref.1) | copy-start | bytes 1572868
  0.6 1.5 %copy-start = (bf16[128,2048]{1,0:T(8,128)(2,1)S(1)}, bf16[128,2048]{1,0:T(8,128)(2,1)}, u32[]{:S(2)}) copy-start(bf16[128,2048]{1,0:T(8,128)(2,1)} %grad_ref.1) | copy-start | bytes 1572868
  2.7 39.9 %copy-start.2 = (bf16[2,256,512]{2,1,0:T(8,128)(2,1)S(1)}, bf16[2,256,512]{2,1,0:T(8,128)(2,1)}, u32[]{:S(2)}) copy-start(bf16[2,256,512]{2,1,0:T(8,128)(2,1)} %constant.5.clone.inverse) | copy-start | bytes 1572868
  2.7 39.9 %copy-start.3 = (bf16[2,512,256]{2,1,0:T(8,128)(2,1)S(1)}, bf16[2,512,256]{2,1,0:T(8,128)(2,1)}, u32[]{:S(2)}) copy-start(bf16[2,512,256]{2,1,0:T(8,128)(2,1)} %constant.4.clone.forward) | copy-start | bytes 1572868

commit v4 on v3

--- a/solution.py
+++ b/solution.py
@@ -32,11 +32,9 @@
 
 
 def inverse_dft(table, spec):
-    head = spec.astype(BF16)
-    tail = (spec - head.astype(F32)).astype(BF16)
-    total = jnp.dot(table[0], head, preferred_element_type=F32)
-    total += jnp.dot(table[1], head, preferred_element_type=F32)
-    return total + jnp.dot(table[0], tail, preferred_element_type=F32)
+    spec = spec.astype(BF16)
+    first = jnp.dot(table[0], spec, preferred_element_type=F32)
+    return first + jnp.dot(table[1], spec, preferred_element_type=F32)
 
 
 def side_by_side(width):
@@ -71,14 +69,12 @@
             if j + 1 < count:
                 next_re, next_im = grad[j + 1]
                 re, im = (re + next_im, im - next_re) if sign > 0 else (re - next_im, im + next_re)
-            window.append((re, im))
+            window.append((re, im, re + im))
+        left = [(re, im, re - im) for re, im in left]
         for a in range(outs):
-            sum_real = sum_imag = None
-            for (lr, li), (wr, wi) in zip(left, window[a:]):
-                re, im = lr * wr + li * wi, lr * wi - li * wr
-                sum_real = re if sum_real is None else sum_real + re
-                sum_imag = im if sum_imag is None else sum_imag + im
-            out_ref[a, real], out_ref[a, imag] = sum_real, sum_imag
+            terms = [[l * w for l, w in zip(*pair)] for pair in zip(left, window[a:])]
+            reals, imags, mixed = (functools.reduce(lambda x, y: x + y, column) for column in zip(*terms))
+            out_ref[a, real], out_ref[a, imag] = reals + imags, mixed - (reals - imags)
 
     def body(sign, first, t, carry):
         at = pl.multiple_of(first + t * 8, 8)
@@ -114,13 +110,6 @@
         step()
 
 
-def fetch(pairs, sems):
-    copies = [pltpu.make_async_copy(far, near, sems.at[k]) for k, (far, near) in enumerate(pairs)]
-    for copy in copies:
-        copy.start()
-    return copies
-
-
 def half_of(ref, rows, half):
     def load(j):
         return jnp.concatenate([ref[2 * j + u, pl.ds(half * rows, rows), :] for u in range(2)], 0)
@@ -129,18 +118,15 @@
 
 
 def both_grads(block, loads, stores, refs):
-    forward, inverse, fv, iv, grad_spec, value_spec, spec, tap_spec, tap_sum, sems = refs
-    copies = fetch([(forward, fv), (inverse, iv)], sems)
+    forward, inverse, grad_spec, value_spec, spec, tap_spec, tap_sum = refs
     (ready_grad, load_grad), (ready_value, load_value), (ready_taps, load_taps) = loads
     ready_grad()
-    copies[0].wait()
-    copies[1].wait()
     ready_taps()
-    run(spectra(fv, block, load_grad, grad_spec))
+    run(spectra(forward, block, load_grad, grad_spec))
     ready_value()
-    run(spectra(fv, block, load_taps, tap_spec))
-    value_steps = spectra(fv, block, load_value, value_spec)
-    grad_steps = invert(iv, block, spec, stores[0])
+    run(spectra(forward, block, load_taps, tap_spec))
+    value_steps = spectra(forward, block, load_value, value_spec)
+    grad_steps = invert(inverse, block, spec, stores[0])
     if len(value_steps) > 8:
         run(value_steps)
         value_steps = ()
@@ -149,7 +135,7 @@
         run(grad_steps)
         grad_steps = ()
     correlate(block, value_spec, grad_spec, tap_sum, grad_steps)
-    run(invert(iv, block, tap_sum, stores[1]))
+    run(invert(inverse, block, tap_sum, stores[1]))
 
 
 def plain_kernel(block, sent_ref, taps_ref, forward, inverse, grad_ref, tap_grad_ref, *refs):
@@ -297,7 +283,7 @@
     forward, inverse = (jnp.asarray(t) for t in dft_tables(block))
     spec = shape((blocks, 2 * block, own), F32)
     tap_spec = shape((tap_blocks, 2 * block, own), F32)
-    scratch = [shape(forward.shape, BF16), shape(inverse.shape, BF16), spec, spec, spec, tap_spec, tap_spec]
+    scratch = [spec, spec, spec, tap_spec, tap_spec]
     flops = 4 * block * block * own * 5 * (blocks + tap_blocks)
     tap_parts = filter_taps.reshape(tap_rows, tap_segs, ch, ctx, own)
 
@@ -313,8 +299,6 @@
             (sent, forward, inverse),
             [shape((2, rows * ctx, own), BF16), shape((ch, rows * tap_segs, own), F32)] + scratch,
             flops,
-            (1, 2),
-            sems=2,
         )
         back = lax.all_to_all(back, ("ctx", "ch"), 0, 0, tiled=True)
         return call_kernel(
@@ -334,8 +318,6 @@
         (sent, tap_all.reshape(taps, own), forward, inverse),
         scratch,
         flops,
-        (2, 3),
-        sems=2,
     )
     back = lax.all_to_all(input_grad, "ctx", 0, 0, tiled=True)
     grad_inputs = back.transpose(1, 0, 2).reshape(rows, width)

time: 71.5 us -> 70.9 us (level)
  no operation moved by 1% of the time
where the time goes in v4:
time: 70.9 us; the launch traced here: 70.7 us
  blocking collectives  63.1 us (89%)
  Pallas kernels  5.42 us (8%)
  local copies, waits for them, and re-layouts  1.48 us (2%)
    all_to_all x1, blocking collectives, shards(): sent = lax.all_to_all(sent, ('ctx', 'ch'), 0, 0, tiled=True)  39.9 us
    all_to_all x1, blocking collectives, shards(): back = lax.all_to_all(back, ('ctx', 'ch'), 0, 0, tiled=True)  23.2 us
    pallas_call x3, Pallas kernels, call_kernel(): pl.pallas_call(body, out_shape=out_shape, in_specs=[away if k in far else...  5.42 us
    reshape x2, local copies, waits for them, and re-layouts, shards(): tap_parts = filter_taps.reshape(tap_rows, tap_segs, ch, ctx, own)  1.45 us

profile of v4, /device:TPU:1, one launch (start us, length us, event | category | flops | bytes accessed | tf_op | source)
XLA Modules:
  0.0 70.7 jit_solution(10949641903020626879)
XLA Ops:
  0.6 0.0 copy-start.1
  0.6 0.0 copy-start
  0.6 1.3 %reshape.10 = bf16[8,4,2,16,128]{4,3,2,1,0:T(8,128)(2,1)S(1)} reshape(bf16[8,4,4096]{2,1,0:T(4,128)(2,1)} %param.7) | data formatting | bytes 524288 | tf_op jit(solution)/shard_map/reshape | solution.py:288
  2.0 0.1 copy.7
  2.1 0.0 copy-done.1
  2.1 0.0 copy-done
  2.1 0.5 shard_map.68
  2.7 0.0 copy-start.2
  2.7 0.0 copy-start.3
  2.7 39.9 %all_to_all.10.sent_ref = bf16[32,160,128]{2,1,0:T(8,128)(2,1)S(1)} all-to-all(bf16[32,160,128]{2,1,0:T(8,128)(2,1)S(1)} %shard_map.68), channel_id=1, replica_groups=mesh['ctx'=16,'ch'=2] {'ctx','ch'}, dimensions={0} | all-to-all | bytes 2621440 | tf_op jit(solution)/shard_map/all_to_all | solution.py:295
  42.6 0.0 copy-done.2
  42.6 0.0 copy-done.3
  42.6 3.5 %shard_map.69 = bf16[32,96,128]{2,1,0:T(8,128)(2,1)S(1)} custom-call(bf16[32,160,128]{2,1,0:T(8,128)(2,1)S(1)} %all_to_all.10.sent_ref, bf16[2,512,256]{2,1,0:T(8,128)(2,1)S(1)} %copy-done.3, bf16[2,256,512]{2,1,0:T(8,128)(2,1)S(1)} %copy-done.2), custom_call_target="tpu_custom_call" | custom-call | flops 2013265920 | bytes 3145728 | tf_op jit(solution)/shard_map/pallas_call | solution.py:260
  46.1 23.2 %all_to_all.11.back_ref = bf16[32,96,128]{2,1,0:T(8,128)(2,1)S(1)} all-to-all(bf16[32,96,128]{2,1,0:T(8,128)(2,1)S(1)} %shard_map.69), channel_id=1, replica_groups=mesh['ctx'=16,'ch'=2] {'ctx','ch'}, dimensions={0} | all-to-all | bytes 1572864 | tf_op jit(solution)/shard_map/all_to_all | solution.py:303
  69.3 1.4 %shard_map.70 = (bf16[128,2048]{1,0:T(8,128)(2,1)}, f32[8,4,4096]{2,1,0:T(4,128)}) custom-call(bf16[32,96,128]{2,1,0:T(8,128)(2,1)S(1)} %all_to_all.11.back_ref), custom_call_target="tpu_custom_call" | custom-call | bytes 1835008 | tf_op jit(solution)/shard_map/pallas_call | solution.py:260
Async XLA Ops:
  0.6 1.5 %copy-start.1 = (bf16[128,2048]{1,0:T(8,128)(2,1)S(1)}, bf16[128,2048]{1,0:T(8,128)(2,1)}, u32[]{:S(2)}) copy-start(bf16[128,2048]{1,0:T(8,128)(2,1)} %value_ref.1) | copy-start | bytes 1572868
  0.6 1.5 %copy-start = (bf16[128,2048]{1,0:T(8,128)(2,1)S(1)}, bf16[128,2048]{1,0:T(8,128)(2,1)}, u32[]{:S(2)}) copy-start(bf16[128,2048]{1,0:T(8,128)(2,1)} %grad_ref.1) | copy-start | bytes 1572868
  2.7 39.9 %copy-start.2 = (bf16[2,256,512]{2,1,0:T(8,128)(2,1)S(1)}, bf16[2,256,512]{2,1,0:T(8,128)(2,1)}, u32[]{:S(2)}) copy-start(bf16[2,256,512]{2,1,0:T(8,128)(2,1)} %constant.5.clone.inverse) | copy-start | bytes 1572868
  2.7 39.9 %copy-start.3 = (bf16[2,512,256]{2,1,0:T(8,128)(2,1)S(1)}, bf16[2,512,256]{2,1,0:T(8,128)(2,1)}, u32[]{:S(2)}) copy-start(bf16[2,512,256]{2,1,0:T(8,128)(2,1)} %constant.4.clone.forward) | copy-start | bytes 1572868

commit v5 on v4

--- a/solution.py
+++ b/solution.py
@@ -100,7 +100,7 @@
         parts = [spec_ref[j + u] for u in range(group)]
         both = inverse_dft(table, jnp.concatenate(parts, 1) if group > 1 else parts[0])
         for u in range(group):
-            store(j + u, both[:, u * width : (u + 1) * width].astype(BF16))
+            store(j + u, both[:, u * width : (u + 1) * width])
 
     return [functools.partial(step, j) for j in range(0, count, group)]
 
@@ -149,10 +149,10 @@
 
     def store_grad(j, result):
         for u in range(2):
-            grad_ref[2 * j + u] = result[u * rows : (u + 1) * rows]
+            grad_ref[2 * j + u] = result[u * rows : (u + 1) * rows].astype(BF16)
 
     def store_taps(j, result):
-        tap_grad_ref[pl.ds(j * block, block), :] = result
+        tap_grad_ref[pl.ds(j * block, block), :] = result.astype(BF16)
 
     both_grads(block, loads, (store_grad, store_taps), (forward, inverse, *refs))
 
@@ -172,12 +172,12 @@
     for i in range(out_ref.shape[0] // 2):
         columns = pl.ds(i * own, own)
         for n, ref in enumerate((grad_ref, value_ref)):
-            pair = traded(ref[pl.ds(0, half), columns].astype(F32), ref[pl.ds(half, half), columns].astype(F32))
+            pair = traded(ref[pl.ds(0, half), columns], ref[pl.ds(half, half), columns])
             for j in range(2):
-                out_ref[2 * i + j, pl.ds(n * half, half), :] = pair[j].astype(BF16)
-        pair = traded(taps_ref[0, i].astype(F32), taps_ref[1, i].astype(F32))
+                out_ref[2 * i + j, pl.ds(n * half, half), :] = pair[j]
+        pair = traded(taps_ref[0, i], taps_ref[1, i])
         for j in range(2):
-            out_ref[2 * i + j, pl.ds(2 * half, size), :] = pair[j].astype(BF16)
+            out_ref[2 * i + j, pl.ds(2 * half, size), :] = pair[j]
 
 
 def paired_kernel(sizes, sent_ref, forward, inverse, out_ref, whole, taps, *refs):
@@ -187,9 +187,9 @@
 
     def untrade(n):
         for i in range(count):
-            pair = [sent_ref[2 * i + j, pl.ds(n * half, half), :].astype(F32) for j in range(2)]
+            pair = [sent_ref[2 * i + j, pl.ds(n * half, half), :] for j in range(2)]
             for u, part in enumerate(traded(*pair)):
-                whole[n, pl.ds(i * rows + u * half, half), :] = part.astype(BF16)
+                whole[n, pl.ds(i * rows + u * half, half), :] = part
 
     def gather_taps():
         for i in range(count):
@@ -206,16 +206,16 @@
         return s // tap_segs, pl.ds(s % tap_segs, rows, stride=tap_segs), slice(None)
 
     def store_grad(j, result):
+        result = result.astype(BF16)
         for u in range(2):
             at = u * rows
-            result32 = result.astype(F32)
-            pair = traded(result32[at : at + half], result32[at + half : at + rows])
+            pair = traded(result[at : at + half], result[at + half : at + rows])
             for side in range(2):
-                out_ref[2 * (2 * j + u) + side, pl.ds(0, half), :] = pair[side].astype(BF16)
+                out_ref[2 * (2 * j + u) + side, pl.ds(0, half), :] = pair[side]
 
     def store_taps(j, result):
         for u in range(2):
-            taps[segment(2 * j + u)] = result[u * rows : (u + 1) * rows].astype(F32)
+            taps[segment(2 * j + u)] = result[u * rows : (u + 1) * rows]
         if (2 * j + 2) % tap_segs:
             return
         side = 2 * j // tap_segs
@@ -231,12 +231,12 @@
     tap_rows, tap_segs = taps_ref.shape[:2]
     size = tap_rows * tap_segs
     for i in range(back_ref.shape[0] // 2):
-        pair = traded(*[back_ref[2 * i + j, pl.ds(0, half), :].astype(F32) for j in range(2)])
+        pair = traded(*[back_ref[2 * i + j, pl.ds(0, half), :] for j in range(2)])
         for u in range(2):
-            grad_ref[pl.ds(u * half, half), pl.ds(i * own, own)] = pair[u].astype(BF16)
-        pair = traded(*[back_ref[2 * i + j, pl.ds(half, size), :].astype(F32) for j in range(2)])
+            grad_ref[pl.ds(u * half, half), pl.ds(i * own, own)] = pair[u]
+        pair = traded(*[back_ref[2 * i + j, pl.ds(half, size), :] for j in range(2)])
         for side in range(2):
-            taps_ref[:, :, pl.ds(side * width + i * own, own)] = pair[side].reshape(tap_rows, tap_segs, own)
+            taps_ref[:, :, pl.ds(side * width + i * own, own)] = pair[side].astype(F32).reshape(tap_rows, tap_segs, own)
 
 
 def split_kernel(*refs):

time: 70.9 us -> 70.7 us (level)
  no operation moved by 1% of the time
where the time goes in v5:
time: 70.7 us; the launch traced here: 70.5 us
  blocking collectives  63.1 us (89%)
  Pallas kernels  5.2 us (7%)
  local copies, waits for them, and re-layouts  1.48 us (2%)
  between operations  0.71 us (1%)
    all_to_all x1, blocking collectives, shards(): sent = lax.all_to_all(sent, ('ctx', 'ch'), 0, 0, tiled=True)  39.9 us
    all_to_all x1, blocking collectives, shards(): back = lax.all_to_all(back, ('ctx', 'ch'), 0, 0, tiled=True)  23.2 us
    pallas_call x3, Pallas kernels, call_kernel(): pl.pallas_call(body, out_shape=out_shape, in_specs=[away if k in far else...  5.2 us
    reshape x2, local copies, waits for them, and re-layouts, shards(): tap_parts = filter_taps.reshape(tap_rows, tap_segs, ch, ctx, own)  1.45 us

profile of v5, /device:TPU:1, one launch (start us, length us, event | category | flops | bytes accessed | tf_op | source)
XLA Modules:
  0.0 70.5 jit_solution(14609822626815942457)
XLA Ops:
  0.6 0.0 copy-start.1
  0.6 0.0 copy-start
  0.6 1.3 %reshape.10 = bf16[8,4,2,16,128]{4,3,2,1,0:T(8,128)(2,1)S(1)} reshape(bf16[8,4,4096]{2,1,0:T(4,128)(2,1)} %param.7) | data formatting | bytes 524288 | tf_op jit(solution)/shard_map/reshape | solution.py:288
  2.0 0.1 copy.7
  2.1 0.0 copy-done.1
  2.1 0.0 copy-done
  2.1 0.4 shard_map.68
  2.6 0.0 copy-start.2
  2.6 0.0 copy-start.3
  2.6 39.9 %all_to_all.10.sent_ref = bf16[32,160,128]{2,1,0:T(8,128)(2,1)S(1)} all-to-all(bf16[32,160,128]{2,1,0:T(8,128)(2,1)S(1)} %shard_map.68), channel_id=1, replica_groups=mesh['ctx'=16,'ch'=2] {'ctx','ch'}, dimensions={0} | all-to-all | bytes 2621440 | tf_op jit(solution)/shard_map/all_to_all | solution.py:295
  42.5 0.0 copy-done.2
  42.5 0.0 copy-done.3
  42.5 3.5 %shard_map.69 = bf16[32,96,128]{2,1,0:T(8,128)(2,1)S(1)} custom-call(bf16[32,160,128]{2,1,0:T(8,128)(2,1)S(1)} %all_to_all.10.sent_ref, bf16[2,512,256]{2,1,0:T(8,128)(2,1)S(1)} %copy-done.3, bf16[2,256,512]{2,1,0:T(8,128)(2,1)S(1)} %copy-done.2), custom_call_target="tpu_custom_call" | custom-call | flops 2013265920 | bytes 3145728 | tf_op jit(solution)/shard_map/pallas_call | solution.py:260
  46.0 23.2 %all_to_all.11.back_ref = bf16[32,96,128]{2,1,0:T(8,128)(2,1)S(1)} all-to-all(bf16[32,96,128]{2,1,0:T(8,128)(2,1)S(1)} %shard_map.69), channel_id=1, replica_groups=mesh['ctx'=16,'ch'=2] {'ctx','ch'}, dimensions={0} | all-to-all | bytes 1572864 | tf_op jit(solution)/shard_map/all_to_all | solution.py:303
  69.2 1.3 %shard_map.70 = (bf16[128,2048]{1,0:T(8,128)(2,1)}, f32[8,4,4096]{2,1,0:T(4,128)}) custom-call(bf16[32,96,128]{2,1,0:T(8,128)(2,1)S(1)} %all_to_all.11.back_ref), custom_call_target="tpu_custom_call" | custom-call | bytes 1835008 | tf_op jit(solution)/shard_map/pallas_call | solution.py:260
Async XLA Ops:
  0.6 1.5 %copy-start.1 = (bf16[128,2048]{1,0:T(8,128)(2,1)S(1)}, bf16[128,2048]{1,0:T(8,128)(2,1)}, u32[]{:S(2)}) copy-start(bf16[128,2048]{1,0:T(8,128)(2,1)} %value_ref.1) | copy-start | bytes 1572868
  0.6 1.5 %copy-start = (bf16[128,2048]{1,0:T(8,128)(2,1)S(1)}, bf16[128,2048]{1,0:T(8,128)(2,1)}, u32[]{:S(2)}) copy-start(bf16[128,2048]{1,0:T(8,128)(2,1)} %grad_ref.1) | copy-start | bytes 1572868
  2.6 39.9 %copy-start.2 = (bf16[2,256,512]{2,1,0:T(8,128)(2,1)S(1)}, bf16[2,256,512]{2,1,0:T(8,128)(2,1)}, u32[]{:S(2)}) copy-start(bf16[2,256,512]{2,1,0:T(8,128)(2,1)} %constant.5.clone.inverse) | copy-start | bytes 1572868
  2.6 39.9 %copy-start.3 = (bf16[2,512,256]{2,1,0:T(8,128)(2,1)S(1)}, bf16[2,512,256]{2,1,0:T(8,128)(2,1)}, u32[]{:S(2)}) copy-start(bf16[2,512,256]{2,1,0:T(8,128)(2,1)} %constant.4.clone.forward) | copy-start | bytes 1572868

commit v6 on v5

--- a/solution.py
+++ b/solution.py
@@ -23,7 +23,7 @@
     turns = ((2 * freq[:, None] + 1) * np.arange(block)[None, :]) % (4 * block)
     angle = turns * (np.pi / (2 * block))
     forward = np.concatenate([np.cos(angle), -np.sin(angle)], 0)
-    return two_bf16(forward), two_bf16(forward.T / block)
+    return two_bf16(forward), (forward.T / block).astype(np.float32).astype(jnp.bfloat16)
 
 
 def forward_dft(table, columns):
@@ -32,9 +32,7 @@
 
 
 def inverse_dft(table, spec):
-    spec = spec.astype(BF16)
-    first = jnp.dot(table[0], spec, preferred_element_type=F32)
-    return first + jnp.dot(table[1], spec, preferred_element_type=F32)
+    return jnp.dot(table[...], spec.astype(BF16), preferred_element_type=F32)
 
 
 def side_by_side(width):
@@ -120,11 +118,11 @@
 def both_grads(block, loads, stores, refs):
     forward, inverse, grad_spec, value_spec, spec, tap_spec, tap_sum = refs
     (ready_grad, load_grad), (ready_value, load_value), (ready_taps, load_taps) = loads
+    ready_taps()
+    run(spectra(forward, block, load_taps, tap_spec))
     ready_grad()
-    ready_taps()
     run(spectra(forward, block, load_grad, grad_spec))
     ready_value()
-    run(spectra(forward, block, load_taps, tap_spec))
     value_steps = spectra(forward, block, load_value, value_spec)
     grad_steps = invert(inverse, block, spec, stores[0])
     if len(value_steps) > 8:

time: 70.7 us -> 70.3 us (level)
  no operation moved by 1% of the time
where the time goes in v6:
time: 70.3 us; the launch traced here: 70.1 us
  blocking collectives  63.1 us (90%)
  Pallas kernels  4.86 us (7%)
  local copies, waits for them, and re-layouts  1.48 us (2%)
  between operations  0.71 us (1%)
    all_to_all x1, blocking collectives, shards(): sent = lax.all_to_all(sent, ('ctx', 'ch'), 0, 0, tiled=True)  39.9 us
    all_to_all x1, blocking collectives, shards(): back = lax.all_to_all(back, ('ctx', 'ch'), 0, 0, tiled=True)  23.2 us
    pallas_call x3, Pallas kernels, call_kernel(): pl.pallas_call(body, out_shape=out_shape, in_specs=[away if k in far else...  4.86 us
    reshape x2, local copies, waits for them, and re-layouts, shards(): tap_parts = filter_taps.reshape(tap_rows, tap_segs, ch, ctx, own)  1.45 us

profile of v6, /device:TPU:1, one launch (start us, length us, event | category | flops | bytes accessed | tf_op | source)
XLA Modules:
  0.0 70.1 jit_solution(8246668566501479447)
XLA Ops:
  0.6 0.0 copy-start.1
  0.6 0.0 copy-start
  0.6 1.3 %reshape.10 = bf16[8,4,2,16,128]{4,3,2,1,0:T(8,128)(2,1)S(1)} reshape(bf16[8,4,4096]{2,1,0:T(4,128)(2,1)} %param.7) | data formatting | bytes 524288 | tf_op jit(solution)/shard_map/reshape | solution.py:286
  2.0 0.1 copy.7
  2.1 0.0 copy-done.1
  2.1 0.0 copy-done
  2.1 0.4 shard_map.68
  2.6 0.0 copy-start.2
  2.6 0.0 copy-start.3
  2.6 39.9 %all_to_all.10.sent_ref = bf16[32,160,128]{2,1,0:T(8,128)(2,1)S(1)} all-to-all(bf16[32,160,128]{2,1,0:T(8,128)(2,1)S(1)} %shard_map.68), channel_id=1, replica_groups=mesh['ctx'=16,'ch'=2] {'ctx','ch'}, dimensions={0} | all-to-all | bytes 2621440 | tf_op jit(solution)/shard_map/all_to_all | solution.py:293
  42.5 0.0 copy-done.2
  42.5 0.0 copy-done.3
  42.5 3.2 %shard_map.69 = bf16[32,96,128]{2,1,0:T(8,128)(2,1)S(1)} custom-call(bf16[32,160,128]{2,1,0:T(8,128)(2,1)S(1)} %all_to_all.10.sent_ref, bf16[2,512,256]{2,1,0:T(8,128)(2,1)S(1)} %copy-done.2, bf16[256,512]{1,0:T(8,128)(2,1)S(1)} %copy-done.3), custom_call_target="tpu_custom_call" | custom-call | flops 2013265920 | bytes 2883584 | tf_op jit(solution)/shard_map/pallas_call | solution.py:258
  45.7 23.2 %all_to_all.11.back_ref = bf16[32,96,128]{2,1,0:T(8,128)(2,1)S(1)} all-to-all(bf16[32,96,128]{2,1,0:T(8,128)(2,1)S(1)} %shard_map.69), channel_id=1, replica_groups=mesh['ctx'=16,'ch'=2] {'ctx','ch'}, dimensions={0} | all-to-all | bytes 1572864 | tf_op jit(solution)/shard_map/all_to_all | solution.py:301
  68.9 1.3 %shard_map.70 = (bf16[128,2048]{1,0:T(8,128)(2,1)}, f32[8,4,4096]{2,1,0:T(4,128)}) custom-call(bf16[32,96,128]{2,1,0:T(8,128)(2,1)S(1)} %all_to_all.11.back_ref), custom_call_target="tpu_custom_call" | custom-call | bytes 1835008 | tf_op jit(solution)/shard_map/pallas_call | solution.py:258
Async XLA Ops:
  0.6 1.5 %copy-start.1 = (bf16[128,2048]{1,0:T(8,128)(2,1)S(1)}, bf16[128,2048]{1,0:T(8,128)(2,1)}, u32[]{:S(2)}) copy-start(bf16[128,2048]{1,0:T(8,128)(2,1)} %value_ref.1) | copy-start | bytes 1572868
  0.6 1.5 %copy-start = (bf16[128,2048]{1,0:T(8,128)(2,1)S(1)}, bf16[128,2048]{1,0:T(8,128)(2,1)}, u32[]{:S(2)}) copy-start(bf16[128,2048]{1,0:T(8,128)(2,1)} %grad_ref.1) | copy-start | bytes 1572868
  2.6 39.9 %copy-start.2 = (bf16[2,512,256]{2,1,0:T(8,128)(2,1)S(1)}, bf16[2,512,256]{2,1,0:T(8,128)(2,1)}, u32[]{:S(2)}) copy-start(bf16[2,512,256]{2,1,0:T(8,128)(2,1)} %constant.4.clone.forward) | copy-start | bytes 1572868
  2.6 39.9 %copy-start.3 = (bf16[256,512]{1,0:T(8,128)(2,1)S(1)}, bf16[256,512]{1,0:T(8,128)(2,1)}, u32[]{:S(2)}) copy-start(bf16[256,512]{1,0:T(8,128)(2,1)} %constant.5.clone.inverse) | copy-start | bytes 786436

commit v7 on v6

--- a/solution.py
+++ b/solution.py
@@ -1,4 +1,5 @@
 import functools
+import math
 
 import jax
 import jax.numpy as jnp
@@ -223,18 +224,32 @@
     both_grads(block, loads, (store_grad, store_taps), (forward, inverse, *refs))
 
 
-def unpack_kernel(back_ref, grad_ref, taps_ref):
+def unpack_kernel(parts, back_ref, grad_hbm, taps_hbm, grad_ref, taps_ref, sems):
     rows, width = grad_ref.shape
     half, own = rows // 2, back_ref.shape[2]
     tap_rows, tap_segs = taps_ref.shape[:2]
     size = tap_rows * tap_segs
-    for i in range(back_ref.shape[0] // 2):
-        pair = traded(*[back_ref[2 * i + j, pl.ds(0, half), :] for j in range(2)])
-        for u in range(2):
-            grad_ref[pl.ds(u * half, half), pl.ds(i * own, own)] = pair[u]
-        pair = traded(*[back_ref[2 * i + j, pl.ds(half, size), :] for j in range(2)])
+    each = back_ref.shape[0] // 2 // parts
+    copies = []
+
+    def leave(near, far, columns):
+        copies.append(pltpu.make_async_copy(near.at[..., columns], far.at[..., columns], sems.at[len(copies)]))
+        copies[-1].start()
+
+    for n in range(parts):
+        for i in range(n * each, (n + 1) * each):
+            pair = traded(*[back_ref[2 * i + j, pl.ds(0, half), :] for j in range(2)])
+            for u in range(2):
+                grad_ref[pl.ds(u * half, half), pl.ds(i * own, own)] = pair[u]
+            pair = traded(*[back_ref[2 * i + j, pl.ds(half, size), :] for j in range(2)])
+            for side in range(2):
+                tap_part = pair[side].astype(F32).reshape(tap_rows, tap_segs, own)
+                taps_ref[:, :, pl.ds(side * width + i * own, own)] = tap_part
+        leave(grad_ref, grad_hbm, pl.ds(n * each * own, each * own))
         for side in range(2):
-            taps_ref[:, :, pl.ds(side * width + i * own, own)] = pair[side].astype(F32).reshape(tap_rows, tap_segs, own)
+            leave(taps_ref, taps_hbm, pl.ds(side * width + n * each * own, each * own))
+    for copy in copies:
+        copy.wait()
 
 
 def split_kernel(*refs):
@@ -246,9 +261,8 @@
             out_ref[k, pl.ds(n * rows, rows), :] = ref[:, k * own : (k + 1) * own]
 
 
-def call_kernel(body, out_shape, operands, scratch=(), flops=0, far=(), sems=0):
-    held = [a for k, a in enumerate(operands) if k not in far]
-    held += list(out_shape) + list(scratch)
+def call_kernel(body, out_shape, operands, scratch=(), flops=0, far_out=(), sems=0):
+    held = list(operands) + [a for k, a in enumerate(out_shape) if k not in far_out] + list(scratch)
     padded = sum(int(np.prod(a.shape[:-1])) * max(a.shape[-1], 128) * a.dtype.itemsize for a in held)
     moved = sum(int(np.prod(a.shape)) * a.dtype.itemsize for a in list(operands) + list(out_shape))
     near, away = pl.BlockSpec(memory_space=pltpu.VMEM), pl.BlockSpec(memory_space=pl.ANY)
@@ -258,8 +272,8 @@
     return pl.pallas_call(
         body,
         out_shape=out_shape,
-        in_specs=[away if k in far else near for k in range(len(operands))],
-        out_specs=[near] * len(out_shape),
+        in_specs=[near] * len(operands),
+        out_specs=[away if k in far_out else near for k in range(len(out_shape))],
         scratch_shapes=scratch_shapes,
         compiler_params=pltpu.CompilerParams(vmem_limit_bytes=min(padded + (6 << 20), 56 << 20)),
         cost_estimate=pl.CostEstimate(flops=flops, bytes_accessed=moved, transcendentals=0),
@@ -299,10 +313,10 @@
             flops,
         )
         back = lax.all_to_all(back, ("ctx", "ch"), 0, 0, tiled=True)
+        outs = [shape((rows, width), BF16), shape(filter_taps.shape, F32)]
+        parts = math.gcd(ctx, 4)
         return call_kernel(
-            unpack_kernel,
-            [shape((rows, width), BF16), shape(filter_taps.shape, F32)],
-            (back,),
+            functools.partial(unpack_kernel, parts), outs, (back,), outs, far_out=(0, 1), sems=3 * parts
         )
 
     (sent,) = call_kernel(split_kernel, [shape((ctx, 2 * rows, own), BF16)], (grad_out, inputs))

time: 70.3 us -> 70.2 us (level)
  no operation moved by 1% of the time
where the time goes in v7:
time: 70.2 us; the launch traced here: 70 us
  blocking collectives  63.1 us (90%)
  Pallas kernels  4.77 us (7%)
  local copies, waits for them, and re-layouts  1.48 us (2%)
  between operations  0.71 us (1%)
    all_to_all x1, blocking collectives, shards(): sent = lax.all_to_all(sent, ('ctx', 'ch'), 0, 0, tiled=True)  39.9 us
    all_to_all x1, blocking collectives, shards(): back = lax.all_to_all(back, ('ctx', 'ch'), 0, 0, tiled=True)  23.2 us
    pallas_call x3, Pallas kernels, call_kernel(): pl.pallas_call(body, out_shape=out_shape, in_specs=[near] * len(operands)...  4.77 us
    reshape x2, local copies, waits for them, and re-layouts, shards(): tap_parts = filter_taps.reshape(tap_rows, tap_segs, ch, ctx, own)  1.45 us

profile of v7, /device:TPU:1, one launch (start us, length us, event | category | flops | bytes accessed | tf_op | source)
XLA Modules:
  0.0 70.0 jit_solution(820093397776970614)
XLA Ops:
  0.6 0.0 copy-start.1
  0.6 0.0 copy-start
  0.6 1.3 %reshape.10 = bf16[8,4,2,16,128]{4,3,2,1,0:T(8,128)(2,1)S(1)} reshape(bf16[8,4,4096]{2,1,0:T(4,128)(2,1)} %param.7) | data formatting | bytes 524288 | tf_op jit(solution)/shard_map/reshape | solution.py:300
  2.0 0.1 copy.7
  2.1 0.0 copy-done.1
  2.1 0.0 copy-done
  2.1 0.4 shard_map.68
  2.6 0.0 copy-start.2
  2.6 0.0 copy-start.3
  2.6 39.9 %all_to_all.10.sent_ref = bf16[32,160,128]{2,1,0:T(8,128)(2,1)S(1)} all-to-all(bf16[32,160,128]{2,1,0:T(8,128)(2,1)S(1)} %shard_map.68), channel_id=1, replica_groups=mesh['ctx'=16,'ch'=2] {'ctx','ch'}, dimensions={0} | all-to-all | bytes 2621440 | tf_op jit(solution)/shard_map/all_to_all | solution.py:307
  42.5 0.0 copy-done.2
  42.5 0.0 copy-done.3
  42.5 3.2 %shard_map.69 = bf16[32,96,128]{2,1,0:T(8,128)(2,1)S(1)} custom-call(bf16[32,160,128]{2,1,0:T(8,128)(2,1)S(1)} %all_to_all.10.sent_ref, bf16[2,512,256]{2,1,0:T(8,128)(2,1)S(1)} %copy-done.2, bf16[256,512]{1,0:T(8,128)(2,1)S(1)} %copy-done.3), custom_call_target="tpu_custom_call" | custom-call | flops 2013265920 | bytes 2883584 | tf_op jit(solution)/shard_map/pallas_call | solution.py:272
  45.7 23.2 %all_to_all.11.back_ref = bf16[32,96,128]{2,1,0:T(8,128)(2,1)S(1)} all-to-all(bf16[32,96,128]{2,1,0:T(8,128)(2,1)S(1)} %shard_map.69), channel_id=1, replica_groups=mesh['ctx'=16,'ch'=2] {'ctx','ch'}, dimensions={0} | all-to-all | bytes 1572864 | tf_op jit(solution)/shard_map/all_to_all | solution.py:315
  68.9 1.2 %shard_map.70 = (bf16[128,2048]{1,0:T(8,128)(2,1)}, f32[8,4,4096]{2,1,0:T(4,128)}) custom-call(bf16[32,96,128]{2,1,0:T(8,128)(2,1)S(1)} %all_to_all.11.back_ref), custom_call_target="tpu_custom_call" | custom-call | bytes 1835008 | tf_op jit(solution)/shard_map/pallas_call | solution.py:272
Async XLA Ops:
  0.6 1.5 %copy-start.1 = (bf16[128,2048]{1,0:T(8,128)(2,1)S(1)}, bf16[128,2048]{1,0:T(8,128)(2,1)}, u32[]{:S(2)}) copy-start(bf16[128,2048]{1,0:T(8,128)(2,1)} %value_ref.1) | copy-start | bytes 1572868
  0.6 1.5 %copy-start = (bf16[128,2048]{1,0:T(8,128)(2,1)S(1)}, bf16[128,2048]{1,0:T(8,128)(2,1)}, u32[]{:S(2)}) copy-start(bf16[128,2048]{1,0:T(8,128)(2,1)} %grad_ref.1) | copy-start | bytes 1572868
  2.6 39.9 %copy-start.2 = (bf16[2,512,256]{2,1,0:T(8,128)(2,1)S(1)}, bf16[2,512,256]{2,1,0:T(8,128)(2,1)}, u32[]{:S(2)}) copy-start(bf16[2,512,256]{2,1,0:T(8,128)(2,1)} %constant.4.clone.forward) | copy-start | bytes 1572868
  2.6 39.9 %copy-start.3 = (bf16[256,512]{1,0:T(8,128)(2,1)S(1)}, bf16[256,512]{1,0:T(8,128)(2,1)}, u32[]{:S(2)}) copy-start(bf16[256,512]{1,0:T(8,128)(2,1)} %constant.5.clone.inverse) | copy-start | bytes 786436
